TPU v7x, 128 devices: a whole 4x4x4 slice. The times are simulated.
128 devices in a mesh: tm: 32 (over x, y_lo, z), rows: 4 (over y_hi, core).
Axes of the slice: x: 4, y: 4 (y_hi: 2, y_lo: 2; y = y_hi * 2 + y_lo), z: 4, core: 2. Of those that a mesh axis runs over, the one named last changes fastest.
Arguments:
- tokens: bfloat16 [512, 28, 28, 256], P('tm', 'rows')
- region_ids: int32 [512, 28, 28], P('tm', 'rows'), may hold values from 0 to 7, as said below
- gain_attn: float32 [256], replicated, may hold values from 0.25 to 1.75
- qkv_weight: bfloat16 [256, 768], replicated
- proj_weight: bfloat16 [256, 256], replicated, may hold values from -0.375 to 0.375
- gain_mlp: float32 [256], replicated, may hold values from 0.25 to 1.75
- up_weight: bfloat16 [256, 1024], replicated, may hold values from -0.375 to 0.375
- down_weight: bfloat16 [1024, 256], replicated, may hold values from -0.1875 to 0.1875
- gain_merge: float32 [1024], replicated, may hold values from 0.25 to 1.75
- reduce_weight: bfloat16 [1024, 512], replicated, may hold values from -0.1875 to 0.1875
- grad_merged: bfloat16 [512, 14, 14, 512], P(('tm', 'rows')), may hold values from -6 to 6
Outputs:
- merged: bfloat16 [512, 14, 14, 512], P(('tm', 'rows'))
- grad_tokens: bfloat16 [512, 28, 28, 256], P('tm', 'rows')
- grad_qkv: float32 [256, 768], replicated
- grad_proj: float32 [256, 256], replicated
- grad_up: float32 [256, 1024], replicated
- grad_down: float32 [1024, 256], replicated
- grad_reduce: float32 [1024, 512], replicated
- grad_gain_attn: float32 [256], replicated
- grad_gain_mlp: float32 [256], replicated
- grad_gain_merge: float32 [1024], replicated
Inputs may be any that keep to these rules, and one draw needn't show every extreme that they name: `region_ids`: along time, rows and columns every aligned window of 8, 7 and 7 positions has one cut position, possibly at its end; a position's id is 4 a + 2 b + c, where a, b, c are 1 if it lies at or past the cut of its window along time, rows and columns, and 0 otherwise.
All inputs are finite; a program needn't handle non-finite values.
Results may differ from a plain program's by a relative error of at most 0.029.
Values may be sent and summed in bfloat16 or wider, within the bound.
A program may use at most 256 MiB of HBM per device.

v0:
```python
import math

import jax
import jax.numpy as jnp
from jax import lax
from jax.sharding import PartitionSpec as P

HEADS = 8


norm_eps = 1e-05


def shifted(block, axis, distance):
    devices = range(lax.axis_size(axis))
    route = [((i - distance) % len(devices), i) for i in devices]
    return lax.ppermute(block, axis, route)


def norm_forward(values):
    centre = jnp.mean(values, axis=-1, keepdims=True)
    centred = values - centre
    spread = jnp.mean(centred * centred, axis=-1, keepdims=True)
    inverse = lax.rsqrt(spread + norm_eps)
    return (centred * inverse, inverse)


def norm_backward(normed, inverse, gain, incoming):
    gated = incoming * gain
    first_mean = jnp.mean(gated, axis=-1, keepdims=True)
    second_mean = jnp.mean(gated * normed, axis=-1, keepdims=True)
    grad_input = inverse * (gated - first_mean - normed * second_mean)
    grad_gain = jnp.sum(incoming * normed, axis=0)
    return (grad_input, grad_gain)


def contract_rows(left, right):
    return lax.dot_general(
        left, right, (((0,), (0,)), ((), ())), preferred_element_type=jnp.float32
    )


def times_transposed(left, right):
    return lax.dot_general(
        left, right, (((1,), (1,)), ((), ())), preferred_element_type=jnp.float32
    )


def gelu_slope(up_rows):
    normal_cdf = 0.5 * (1.0 + lax.erf(up_rows * 0.7071067811865476))
    normal_pdf = jnp.exp(-0.5 * up_rows * up_rows) * 0.3989422804014327
    return normal_cdf + up_rows * normal_pdf


def to_windows(grid_cells):
    frames, height, across, features = grid_cells.shape
    blocked = grid_cells.reshape(frames // 8, 8, height // 7, 7, across // 7, 7, features)
    return blocked.transpose(0, 2, 4, 1, 3, 5, 6).reshape(-1, 392, features)


def from_windows(windows, frames, height, across):
    features = windows.shape[-1]
    blocked = windows.reshape(frames // 8, height // 7, across // 7, 8, 7, 7, features)
    return blocked.transpose(0, 3, 1, 4, 2, 5, 6).reshape(frames, height, across, features)


def split_heads(qkv_win):
    window_count = qkv_win.shape[0]
    features = qkv_win.shape[-1] // 3
    head_size = features // HEADS
    query_vecs = qkv_win[..., :features].reshape(window_count, 392, HEADS, head_size)
    key_vecs = qkv_win[..., features : 2 * features].reshape(window_count, 392, HEADS, head_size)
    value_vecs = qkv_win[..., 2 * features :].reshape(window_count, 392, HEADS, head_size)
    return (query_vecs, key_vecs, value_vecs, head_size)


def attend_forward(qkv_win, id_win):
    query_vecs, key_vecs, value_vecs, head_size = split_heads(qkv_win)
    scores = jnp.einsum(
        "nqhd,nkhd->nhqk", query_vecs, key_vecs, preferred_element_type=jnp.float32
    ) / math.sqrt(head_size)
    allowed = (id_win[:, :, None] == id_win[:, None, :])[:, None]
    scores = jnp.where(allowed, scores, -1e30)
    row_top = jnp.max(scores, axis=-1, keepdims=True)
    expon = jnp.exp(scores - row_top)
    probs = (expon / jnp.sum(expon, axis=-1, keepdims=True)).astype(jnp.bfloat16)
    attended = jnp.einsum("nhqk,nkhd->nqhd", probs, value_vecs, preferred_element_type=jnp.float32)
    return (attended.astype(jnp.bfloat16).reshape(qkv_win.shape[0], 392, -1), probs)


def attend_backward(qkv_win, probs, grad_att):
    query_vecs, key_vecs, value_vecs, head_size = split_heads(qkv_win)
    window_count = qkv_win.shape[0]
    grad_heads = grad_att.reshape(window_count, 392, HEADS, head_size)
    grad_probs = jnp.einsum(
        "nqhd,nkhd->nhqk", grad_heads, value_vecs, preferred_element_type=jnp.float32
    )
    grad_values = jnp.einsum(
        "nhqk,nqhd->nkhd", probs, grad_heads, preferred_element_type=jnp.float32
    ).astype(jnp.bfloat16)
    probs_wide = probs.astype(jnp.float32)
    inner_sum = jnp.sum(grad_probs * probs_wide, axis=-1, keepdims=True)
    grad_scores = (probs_wide * (grad_probs - inner_sum) / math.sqrt(head_size)).astype(
        jnp.bfloat16
    )
    grad_queries = jnp.einsum(
        "nhqk,nkhd->nqhd", grad_scores, key_vecs, preferred_element_type=jnp.float32
    ).astype(jnp.bfloat16)
    grad_keys = jnp.einsum(
        "nhqk,nqhd->nkhd", grad_scores, query_vecs, preferred_element_type=jnp.float32
    ).astype(jnp.bfloat16)
    pieces = [grad_queries, grad_keys, grad_values]
    return jnp.concatenate([piece.reshape(window_count, 392, -1) for piece in pieces], axis=-1)


def block_forward(
    rolled, region, gain_attn, qkv_weight, proj_weight, gain_mlp, up_weight, down_weight
):
    frames, height, across, features = rolled.shape
    flat = rolled.reshape(-1, features).astype(jnp.float32)
    normed1, inverse1 = norm_forward(flat)
    first_in = (normed1 * gain_attn).astype(jnp.bfloat16)
    qkv_rows = jnp.dot(first_in, qkv_weight, preferred_element_type=jnp.float32).astype(
        jnp.bfloat16
    )
    per_step = across // 7
    qkv_win = to_windows(qkv_rows.reshape(frames, height, across, 3 * features))
    groups = qkv_win.shape[0] // per_step
    qkv_win = qkv_win.reshape(groups, per_step, 392, 3 * features)
    id_win = to_windows(region[..., None])[..., 0].reshape(groups, per_step, 392)

    def attend_group(bundle):
        return attend_forward(bundle[0], bundle[1])

    attended, probs = lax.map(attend_group, (qkv_win, id_win))
    attended = from_windows(attended.reshape(-1, 392, features), frames, height, across).reshape(
        -1, features
    )
    hidden1 = (flat + jnp.dot(attended, proj_weight, preferred_element_type=jnp.float32)).astype(
        jnp.bfloat16
    )
    normed2, inverse2 = norm_forward(hidden1.astype(jnp.float32))
    second_in = (normed2 * gain_mlp).astype(jnp.bfloat16)
    up_rows = jnp.dot(second_in, up_weight, preferred_element_type=jnp.float32)
    act_rows = jax.nn.gelu(up_rows, approximate=False).astype(jnp.bfloat16)
    out_rows = (
        hidden1.astype(jnp.float32)
        + jnp.dot(act_rows, down_weight, preferred_element_type=jnp.float32)
    ).astype(jnp.bfloat16)
    saved = (first_in, qkv_win, probs, attended, hidden1, second_in, up_rows, act_rows)
    return (out_rows.reshape(frames, height, across, features), saved)


def block_backward(
    rolled, saved, grad_out, gain_attn, qkv_weight, proj_weight, gain_mlp, up_weight, down_weight
):
    first_in, qkv_win, probs, attended, hidden1, second_in, up_rows, act_rows = saved
    frames, height, across, features = rolled.shape
    grad_rows = grad_out.reshape(-1, features)
    grad_down = contract_rows(act_rows, grad_rows)
    grad_act = times_transposed(grad_rows, down_weight)
    grad_up_in = (grad_act * gelu_slope(up_rows)).astype(jnp.bfloat16)
    grad_up = contract_rows(second_in, grad_up_in)
    grad_second = times_transposed(grad_up_in, up_weight)
    normed2, inverse2 = norm_forward(hidden1.astype(jnp.float32))
    back_mlp, grad_gain2 = norm_backward(normed2, inverse2, gain_mlp, grad_second)
    grad_hidden = grad_rows.astype(jnp.float32) + back_mlp
    grad_hidden_b = grad_hidden.astype(jnp.bfloat16)
    grad_proj = contract_rows(attended, grad_hidden_b)
    grad_att = times_transposed(grad_hidden_b, proj_weight).astype(jnp.bfloat16)
    att_win = to_windows(grad_att.reshape(frames, height, across, features)).reshape(
        qkv_win.shape[0], qkv_win.shape[1], 392, features
    )

    def attend_group_back(bundle):
        return attend_backward(bundle[0], bundle[1], bundle[2])

    grad_qkv_win = lax.map(attend_group_back, (qkv_win, probs, att_win))
    grad_qkv_rows = from_windows(
        grad_qkv_win.reshape(-1, 392, 3 * features), frames, height, across
    ).reshape(-1, 3 * features)
    grad_qkv = contract_rows(first_in, grad_qkv_rows)
    grad_first = times_transposed(grad_qkv_rows, qkv_weight)
    normed1, inverse1 = norm_forward(rolled.reshape(-1, features).astype(jnp.float32))
    back_attn, grad_gain1 = norm_backward(normed1, inverse1, gain_attn, grad_first)
    grad_input = (grad_hidden + back_attn).astype(jnp.bfloat16)
    return (
        grad_input.reshape(frames, height, across, features),
        (grad_qkv, grad_proj, grad_up, grad_down, grad_gain1, grad_gain2),
    )


def merge_both(section, gain_merge, reduce_weight, grad_merged):
    frames, height, across, features = section.shape
    joined = (
        section.reshape(frames, height // 2, 2, across // 2, 2, features)
        .transpose(0, 1, 3, 4, 2, 5)
        .reshape(-1, 4 * features)
    )
    normed3, inverse3 = norm_forward(joined.astype(jnp.float32))
    third_in = (normed3 * gain_merge).astype(jnp.bfloat16)
    merged = jnp.dot(third_in, reduce_weight, preferred_element_type=jnp.float32).astype(
        jnp.bfloat16
    )
    grad_rows = grad_merged.reshape(-1, reduce_weight.shape[1])
    grad_reduce = contract_rows(third_in, grad_rows)
    grad_third = times_transposed(grad_rows, reduce_weight)
    back_merge, grad_gain3 = norm_backward(normed3, inverse3, gain_merge, grad_third)
    grad_joined = back_merge.astype(jnp.bfloat16)
    grad_section = (
        grad_joined.reshape(frames, height // 2, across // 2, 2, 2, features)
        .transpose(0, 1, 4, 2, 3, 5)
        .reshape(frames, height, across, features)
    )
    return (
        merged.reshape(frames, height // 2, across // 2, -1),
        grad_section,
        grad_reduce,
        grad_gain3,
    )


def local(
    tokens,
    region_ids,
    gain_attn,
    qkv_weight,
    proj_weight,
    gain_mlp,
    up_weight,
    down_weight,
    gain_merge,
    reduce_weight,
    grad_merged,
):
    weights = (gain_attn, qkv_weight, proj_weight, gain_mlp, up_weight, down_weight)
    frames = tokens.shape[0]
    ahead = shifted(tokens[:4], "tm", -1)
    timed = jnp.concatenate([tokens[4:], ahead], axis=0)
    below = shifted(timed[:, :3], "rows", -1)
    rolled = jnp.roll(jnp.concatenate([timed[:, 3:], below], axis=1), -3, axis=2)
    out_rolled, saved = block_forward(rolled, region_ids, *weights)
    back_rows = shifted(out_rolled[:, 4:], "rows", 1)
    partial_rows = jnp.concatenate([back_rows, out_rolled[:, :4]], axis=1)
    back_frames = shifted(partial_rows[frames - 4 :], "tm", 1)
    initial = jnp.roll(
        jnp.concatenate([back_frames, partial_rows[: frames - 4]], axis=0), 3, axis=2
    )
    section = lax.all_to_all(initial, "rows", split_axis=0, concat_axis=1, tiled=True)
    merged, grad_section, grad_reduce, grad_gain3 = merge_both(
        section, gain_merge, reduce_weight, grad_merged
    )
    grad_initial = lax.all_to_all(grad_section, "rows", split_axis=1, concat_axis=0, tiled=True)
    grad_ahead = shifted(grad_initial[:4], "tm", -1)
    grad_timed = jnp.concatenate([grad_initial[4:], grad_ahead], axis=0)
    grad_below = shifted(grad_timed[:, :3], "rows", -1)
    grad_rolled = jnp.roll(jnp.concatenate([grad_timed[:, 3:], grad_below], axis=1), -3, axis=2)
    grad_input, grads = block_backward(rolled, saved, grad_rolled, *weights)
    grad_qkv, grad_proj, grad_up, grad_down, grad_gain1, grad_gain2 = grads
    grad_qkv, grad_proj, grad_up, grad_down, grad_gain1, grad_gain2, grad_reduce, grad_gain3 = (
        lax.psum(
            (
                grad_qkv,
                grad_proj,
                grad_up,
                grad_down,
                grad_gain1,
                grad_gain2,
                grad_reduce,
                grad_gain3,
            ),
            ("tm", "rows"),
        )
    )
    grad_back_rows = shifted(grad_input[:, 4:], "rows", 1)
    grad_partial = jnp.concatenate([grad_back_rows, grad_input[:, :4]], axis=1)
    grad_back_frames = shifted(grad_partial[frames - 4 :], "tm", 1)
    grad_tokens = jnp.roll(
        jnp.concatenate([grad_back_frames, grad_partial[: frames - 4]], axis=0), 3, axis=2
    )
    return (
        merged,
        grad_tokens,
        grad_qkv,
        grad_proj,
        grad_up,
        grad_down,
        grad_reduce,
        grad_gain1,
        grad_gain2,
        grad_gain3,
    )


def solution(mesh):
    placed = (
        P("tm", "rows", None, None),
        P("tm", "rows", None),
        P(),
        P(),
        P(),
        P(),
        P(),
        P(),
        P(),
        P(),
        P(("tm", "rows"), None, None, None),
    )
    return jax.shard_map(
        local,
        mesh=mesh,
        in_specs=placed,
        out_specs=(
            P(("tm", "rows"), None, None, None),
            P("tm", "rows", None, None),
            P(),
            P(),
            P(),
            P(),
            P(),
            P(),
            P(),
            P(),
        ),
        check_vma=False,
    )
```

profile of v0, /device:TPU:1, one launch (start us, length us, event | category | flops | bytes accessed | tf_op | source)
XLA Modules:
  0.0 771.3 jit_solution(15715356887885405792)
XLA Ops:
  29.4 10.6 %collective-permute-done.1 = bf16[16,3,28,256]{3,0,2,1:T(8,128)(2,1)} collective-permute-done((bf16[16,3,28,256]{3,0,2,1:T(8,128)(2,1)}, bf16[16,3,28,256]{3,0,2,1:T(8,128)(2,1)}, u32[]{:S(2)}, u32[]{:S(2)}) %collective-permute-start.1) | collective-permute-done | bytes 688160 | tf_op jit(solution)/shard_map/ppermute | solution.py:17
  72.2 10.1 %copy.100 = bf16[2,4,392,768]{2,3,1,0:T(8,128)(2,1)} copy(bf16[2,4,392,768]{3,1,2,0:T(4,128)(2,1)} %bitcast.191) | data formatting | bytes 9633792 | tf_op jit(solution)/shard_map/while | solution.py:135
  82.3 80.9 %while.22 = (s32[]{:T(128)}, bf16[2,4,392,256]{3,1,2,0:T(4,128)(2,1)}, bf16[2,4,8,392,392]{3,4,2,1,0:T(8,128)(2,1)}, bf16[2,4,392,768]{2,3,1,0:T(8,128)(2,1)}, s32[2,4,392]{2,1,0:T(4,128)S(1)}, /*index=5*/s32[]{:T(128)}) while((s32[]{:T(128)}, bf16[2,4,392,256]{3,1,2,0:T(4,128)(2,1)}, bf16[2,4,8,392,392]{3,4,2,1,0:T(8,128)(2,1)}, ...), condition=%wide.region_5.6_spmd, body=%wide.region_2.5_spmd.sunk | while | flops 659927680 | bytes 95279048 | solution.py:135
  87.3 15.3 %fusion.139 = (f32[4,8,392]{2,1,0:T(8,128)S(1)}, f32[4,8,392,392]{2,3,1,0:T(8,128)}) fusion(pred[4,392,392]{1,2,0:T(8,128)(4,1)} %broadcast_compare_fusion.2, bf16[4,392,8,32]{1,3,2,0:T(8,128)(2,1)} %bitcast.184, bf16[4,392,8,32]{1,3,2,0:T(8,128)(2,1)S(1)} %bitcast.183), kind=kOutput, calls=%fused_computation.157.clone.1 | convolution fusion | flops 334373248 | bytes 21939456 | tf_op jit(solution)/shard_map/while/body/eval_jaxpr/sub | solution.py:85
  102.6 15.9 %bitcast_dynamic-update-slice_fusion.2 = (bf16[2,4,8,392,392]{3,4,2,1,0:T(8,128)(2,1)}, bf16[4,8,392,392]{2,3,1,0:T(8,128)(2,1)S(1)}) fusion(bf16[2,4,8,392,392]{3,4,2,1,0:T(8,128)(2,1)} %get-tuple-element.286, s32[]{:T(128)} %get-tuple-element.284, f32[4,8,392,392]{2,3,1,0:T(8,128)} %get-tuple-element.266, f32[4,8,392]{2,1,0:T(8,128)S(1)} %get-tuple-element.267), kind=kLoop, calls=%fused_computation.5.clone.1 | loop fusion | flops 9834496 | bytes 48420352 | tf_op jit(solution)/shard_map/while/body/jit(dynamic_update_index_in_dim)/dynamic_update_slice | solution.py:135
  127.6 15.3 %fusion.139 = (f32[4,8,392]{2,1,0:T(8,128)S(1)}, f32[4,8,392,392]{2,3,1,0:T(8,128)}) fusion(pred[4,392,392]{1,2,0:T(8,128)(4,1)} %broadcast_compare_fusion.2, bf16[4,392,8,32]{1,3,2,0:T(8,128)(2,1)} %bitcast.184, bf16[4,392,8,32]{1,3,2,0:T(8,128)(2,1)S(1)} %bitcast.183), kind=kOutput, calls=%fused_computation.157.clone.1 | convolution fusion | flops 334373248 | bytes 21939456 | tf_op jit(solution)/shard_map/while/body/eval_jaxpr/sub | solution.py:85
  142.9 15.9 %bitcast_dynamic-update-slice_fusion.2 = (bf16[2,4,8,392,392]{3,4,2,1,0:T(8,128)(2,1)}, bf16[4,8,392,392]{2,3,1,0:T(8,128)(2,1)S(1)}) fusion(bf16[2,4,8,392,392]{3,4,2,1,0:T(8,128)(2,1)} %get-tuple-element.286, s32[]{:T(128)} %get-tuple-element.284, f32[4,8,392,392]{2,3,1,0:T(8,128)} %get-tuple-element.266, f32[4,8,392]{2,1,0:T(8,128)S(1)} %get-tuple-element.267), kind=kLoop, calls=%fused_computation.5.clone.1 | loop fusion | flops 9834496 | bytes 48420352 | tf_op jit(solution)/shard_map/while/body/jit(dynamic_update_index_in_dim)/dynamic_update_slice | solution.py:135
  173.7 32.0 %fusion.36 = (bf16[3136,1024]{1,0:T(8,128)(2,1)S(1)}, f32[3136,1024]{1,0:T(8,128)}) fusion(bf16[256,1024]{1,0:T(8,128)(2,1)S(1)} %copy-done.52, f32[3136,256]{1,0:T(8,128)S(1)} %get-tuple-element.188, f32[256]{0:T(256)S(1)} %copy-done.47, f32[3136]{0:T(1024)S(1)} %add_rsqrt_fusion.2, f32[3136]{0:T(1024)S(1)} %broadcast_multiply_fusion.6), kind=kOutput, calls=%fused_computation.48 | convolution fusion | flops 1856110592 | bytes 23029248 | tf_op jit(solution)/shard_map/dot_general | solution.py:144
  222.4 13.6 %collective-permute-done.3 = bf16[4,7,28,256]{3,2,1,0:T(8,128)(2,1)S(1)} collective-permute-done((bf16[4,7,28,256]{3,2,1,0:T(8,128)(2,1)S(1)}, bf16[4,7,28,256]{3,2,1,0:T(8,128)(2,1)S(1)}, u32[]{:S(2)}, u32[]{:S(2)}) %collective-permute-start.3) | collective-permute-done | bytes 401440 | tf_op jit(solution)/shard_map/ppermute | solution.py:17
  250.4 18.8 %all-to-all-done = bf16[16,7,28,256]{3,2,1,0:T(8,128)(2,1)S(1)} async-done(((bf16[16,7,28,256]{3,2,1,0:T(8,128)(2,1)}), bf16[16,7,28,256]{3,2,1,0:T(8,128)(2,1)S(1)}, u32[]{:S(2)}, u32[]{:S(2)}) %all-to-all-start) | async-done | bytes 1605664 | tf_op jit(solution)/shard_map/all_to_all | solution.py:249
  298.1 24.7 %all_to_all.27 = bf16[4,28,28,256]{3,0,2,1:T(4,128)(2,1)S(1)} all-to-all(bf16[4,28,28,256]{3,0,2,1:T(4,128)(2,1)S(1)} %bitcast.198), channel_id=1, replica_groups=mesh['tm'=32,'rows'=4] {'rows'}, dimensions={1} | all-to-all | bytes 3211264 | tf_op jit(solution)/shard_map/all_to_all | solution.py:253
  362.9 10.0 %fusion.42 = bf16[3136,1024]{1,0:T(8,128)(2,1)S(1)} fusion(f32[3136,1024]{1,0:T(8,128)} %get-tuple-element.190, bf16[3136,256]{1,0:T(8,128)(2,1)S(1)} %reshape.289, bf16[1024,256]{1,0:T(8,128)(2,1)S(1)} %copy-done.51), kind=kOutput, calls=%fused_computation.54 | convolution fusion | flops 1676279808 | bytes 21397504 | tf_op jit(solution)/shard_map/dot_general | solution.py:44
  390.6 175.6 %while.23 = (s32[]{:T(128)}, bf16[2,4,392,768]{3,1,2,0:T(4,128)(2,1)}, bf16[2,4,392,768]{2,3,1,0:T(8,128)(2,1)}, bf16[2,4,8,392,392]{3,4,2,1,0:T(8,128)(2,1)}, bf16[2,4,392,256]{3,1,2,0:T(4,128)(2,1)}, /*index=5*/s32[]{:T(128)}) while((s32[]{:T(128)}, bf16[2,4,392,768]{3,1,2,0:T(4,128)(2,1)}, bf16[2,4,392,768]{2,3,1,0:T(8,128)(2,1)}, ...), condition=%wide.region_16.17_spmd, body=%wide.region_14.16_spmd.sunk | while | flops 1336112384 | bytes 236678336 | solution.py:178
  397.6 10.4 %fusion.148 = f32[4,8,392,392]{2,3,1,0:T(8,128)} fusion(bf16[4,392,8,32]{1,3,2,0:T(8,128)(2,1)S(1)} %bitcast.173, bf16[4,392,8,32]{1,3,2,0:T(8,128)(2,1)S(1)} %bitcast.178), kind=kOutput, calls=%fused_computation.159.clone.1 | convolution fusion | flops 314703872 | bytes 21274624 | tf_op jit(solution)/shard_map/while/body/eval_jaxpr/nqhd,nkhd->nhqk/dot_general | solution.py:95
  408.0 26.8 %fusion.150 = bf16[4,8,32,392]{3,2,1,0:T(8,128)(2,1)} fusion(bf16[4,392,8,32]{1,3,2,0:T(8,128)(2,1)} %bitcast.186, f32[4,8,392,392]{2,3,1,0:T(8,128)} %fusion.148, bf16[2,4,8,392,392]{3,4,2,1,0:T(8,128)(2,1)} %get-tuple-element.311, s32[]{:T(128)} %get-tuple-element.302), kind=kOutput, calls=%fused_computation.32.clone.1 | convolution fusion | flops 349538944 | bytes 78922752 | tf_op jit(solution)/shard_map/while/body/eval_jaxpr/nhqk,nkhd->nqhd/dot_general | solution.py:106
  434.9 26.6 %fusion.149 = bf16[4,8,32,392]{3,2,1,0:T(8,128)(2,1)} fusion(bf16[4,392,8,32]{1,3,2,0:T(8,128)(2,1)S(1)} %bitcast.185, f32[4,8,392,392]{2,3,1,0:T(8,128)} %fusion.148, bf16[2,4,8,392,392]{3,4,2,1,0:T(8,128)(2,1)} %get-tuple-element.311, s32[]{:T(128)} %get-tuple-element.302), kind=kOutput, calls=%fused_computation.33.clone.1 | convolution fusion | flops 349538944 | bytes 78676992 | tf_op jit(solution)/shard_map/while/body/eval_jaxpr/nhqk,nqhd->nkhd/dot_general | solution.py:109
  485.3 10.4 %fusion.148 = f32[4,8,392,392]{2,3,1,0:T(8,128)} fusion(bf16[4,392,8,32]{1,3,2,0:T(8,128)(2,1)S(1)} %bitcast.173, bf16[4,392,8,32]{1,3,2,0:T(8,128)(2,1)S(1)} %bitcast.178), kind=kOutput, calls=%fused_computation.159.clone.1 | convolution fusion | flops 314703872 | bytes 21274624 | tf_op jit(solution)/shard_map/while/body/eval_jaxpr/nqhd,nkhd->nhqk/dot_general | solution.py:95
  495.7 26.8 %fusion.150 = bf16[4,8,32,392]{3,2,1,0:T(8,128)(2,1)} fusion(bf16[4,392,8,32]{1,3,2,0:T(8,128)(2,1)} %bitcast.186, f32[4,8,392,392]{2,3,1,0:T(8,128)} %fusion.148, bf16[2,4,8,392,392]{3,4,2,1,0:T(8,128)(2,1)} %get-tuple-element.311, s32[]{:T(128)} %get-tuple-element.302), kind=kOutput, calls=%fused_computation.32.clone.1 | convolution fusion | flops 349538944 | bytes 78922752 | tf_op jit(solution)/shard_map/while/body/eval_jaxpr/nhqk,nkhd->nqhd/dot_general | solution.py:106
  522.5 26.5 %fusion.149 = bf16[4,8,32,392]{3,2,1,0:T(8,128)(2,1)} fusion(bf16[4,392,8,32]{1,3,2,0:T(8,128)(2,1)S(1)} %bitcast.185, f32[4,8,392,392]{2,3,1,0:T(8,128)} %fusion.148, bf16[2,4,8,392,392]{3,4,2,1,0:T(8,128)(2,1)} %get-tuple-element.311, s32[]{:T(128)} %get-tuple-element.302), kind=kOutput, calls=%fused_computation.33.clone.1 | convolution fusion | flops 349538944 | bytes 78676992 | tf_op jit(solution)/shard_map/while/body/eval_jaxpr/nhqk,nqhd->nkhd/dot_general | solution.py:109
  549.0 8.4 %fusion.146 = bf16[4,8,32,392]{3,2,1,0:T(8,128)(2,1)S(1)} fusion(bf16[4,392,8,32]{1,3,2,0:T(8,128)(2,1)S(1)} %bitcast.174, bf16[2,4,8,392,392]{3,4,2,1,0:T(8,128)(2,1)} %get-tuple-element.311, s32[]{:T(128)} %get-tuple-element.302), kind=kOutput, calls=%fused_computation.34.clone.1 | convolution fusion | flops 315105280 | bytes 14451200 | tf_op jit(solution)/shard_map/while/body/eval_jaxpr/nhqk,nqhd->nkhd/dot_general | solution.py:98
  572.4 8.6 %reshape_reshape.31 = bf16[3136,768]{1,0:T(8,128)(2,1)} reshape(bf16[2,8,1,7,4,7,768]{6,5,4,3,1,0,2:T(8,128)(2,1)} %copy.119) | data formatting | bytes 9633792 | tf_op jit(solution)/shard_map/reshape;reshape | solution.py:181
  603.7 9.5 %collective-permute-done.6 = bf16[16,3,28,256]{3,0,2,1:T(8,128)(2,1)S(1)} collective-permute-done((bf16[16,3,28,256]{3,0,2,1:T(8,128)(2,1)S(1)}, bf16[16,3,28,256]{3,0,2,1:T(8,128)(2,1)S(1)}, u32[]{:S(2)}, u32[]{:S(2)}) %collective-permute-start.6) | collective-permute-done | bytes 688160 | tf_op jit(solution)/shard_map/ppermute | solution.py:17
  621.2 69.7 %all-reduce = (f32[256]{0:T(256)}, f32[256]{0:T(256)}, f32[1024]{0:T(1024)}) all-reduce(f32[256]{0:T(256)S(1)} %get-tuple-element.140, f32[256]{0:T(256)S(1)} %copy-done.49, f32[1024]{0:T(1024)S(1)} %copy-done.46), channel_id=1, replica_groups=mesh['tm'=32,'rows'=4] {'tm','rows'}, use_global_device_ids=true, to_apply=%region_25.26 | all-reduce | flops 1536 | bytes 12288 | tf_op jit(solution)/shard_map/psum | solution.py:261
  694.0 61.7 %all-reduce.4.cloned.1.call-done = (f32[256,768]{1,0:T(8,128)}, f32[256,256]{1,0:T(8,128)}, f32[256,1024]{1,0:T(8,128)}, f32[1024,256]{1,0:T(8,128)}, f32[1024,512]{1,0:T(8,128)}) async-done(((f32[256,768]{1,0:T(8,128)}, f32[256,256]{1,0:T(8,128)}, f32[256,1024]{1,0:T(8,128)}, f32[1024,256]{1,0:T(8,128)}, f32[1024,512]{1,0:T(8,128)}), (f32[256,768]{1,0:T(8,128)}, f32[256,256]{1,0:T(8,128)}, ...) | async-done | bytes 5242896 | tf_op jit(solution)/shard_map/psum | solution.py:261
  (271 shorter events, 287.9 us)
Async XLA Ops:
  7.2 281.1 %copy-start = (bf16[1024,512]{1,0:T(8,128)(2,1)S(1)}, bf16[1024,512]{1,0:T(8,128)(2,1)}, u32[]{:S(2)}) copy-start(bf16[1024,512]{1,0:T(8,128)(2,1)} %param.24) | copy-start | bytes 3145732
  8.6 20.0 %copy-start.36 = (s32[16,7,28]{2,0,1:T(8,128)S(1)}, s32[16,7,28]{2,0,1:T(8,128)}, u32[]{:S(2)}) copy-start(s32[16,7,28]{2,0,1:T(8,128)} %param.16) | copy-start | bytes 37636
  8.6 17.1 %collective-permute-start = (bf16[4,7,28,256]{3,2,1,0:T(8,128)(2,1)S(1)}, bf16[4,7,28,256]{3,2,1,0:T(8,128)(2,1)S(1)}, u32[]{:S(2)}, u32[]{:S(2)}) collective-permute-start(bf16[4,7,28,256]{3,2,1,0:T(8,128)(2,1)S(1)} %copy.136), channel_id=1, source_target_pairs={{4,0},{8,4},{12,8},{16,12},{20,16},{24,20},{28,24},{32,28},{36,32}... | collective-permute-start | bytes 1204232 | tf_op jit(solution)/shard_map/ppermute | solution.py:17
  27.0 13.0 %collective-permute-start.1 = (bf16[16,3,28,256]{3,0,2,1:T(8,128)(2,1)}, bf16[16,3,28,256]{3,0,2,1:T(8,128)(2,1)}, u32[]{:S(2)}, u32[]{:S(2)}) collective-permute-start(bf16[16,3,28,256]{3,0,2,1:T(8,128)(2,1)} %pad_maximum_fusion.11), channel_id=1, source_target_pairs={{1,0},{2,1},{3,2},{0,3},{5,4},{6,5},{7,6},{4,7},{9,8},{10,9},{11,1... | collective-permute-start | bytes 2064392 | tf_op jit(solution)/shard_map/ppermute | solution.py:17
  172.2 33.5 %copy-start.4 = (f32[3136,256]{1,0:T(8,128)}, f32[3136,256]{1,0:T(8,128)S(1)}, u32[]{:S(2)}) copy-start(f32[3136,256]{1,0:T(8,128)S(1)} %get-tuple-element.188) | copy-start | bytes 9633796
  173.7 34.6 %copy-start.50 = (bf16[1024,256]{1,0:T(8,128)(2,1)S(1)}, bf16[1024,256]{1,0:T(8,128)(2,1)}, u32[]{:S(2)}) copy-start(bf16[1024,256]{1,0:T(8,128)(2,1)} %param.22) | copy-start | bytes 1572868
  214.1 8.0 %collective-permute-start.2 = (bf16[16,3,28,256]{3,0,2,1:T(8,128)(2,1)S(1)}, bf16[16,3,28,256]{3,0,2,1:T(8,128)(2,1)S(1)}, u32[]{:S(2)}, u32[]{:S(2)}) collective-permute-start(bf16[16,3,28,256]{3,0,2,1:T(8,128)(2,1)S(1)} %copy.103), channel_id=1, source_target_pairs={{3,0},{0,1},{1,2},{2,3},{7,4},{4,5},{5,6},{6,7},{11,8},{8,9},{9,10... | collective-permute-start | bytes 2064392 | tf_op jit(solution)/shard_map/ppermute | solution.py:17
  222.4 13.6 %collective-permute-start.3 = (bf16[4,7,28,256]{3,2,1,0:T(8,128)(2,1)S(1)}, bf16[4,7,28,256]{3,2,1,0:T(8,128)(2,1)S(1)}, u32[]{:S(2)}, u32[]{:S(2)}) collective-permute-start(bf16[4,7,28,256]{3,2,1,0:T(8,128)(2,1)S(1)} %pad_maximum_fusion.13), channel_id=1, source_target_pairs={{124,0},{0,4},{4,8},{8,12},{12,16},{16,20},{20,24},{24,28},{28,32}... | collective-permute-start | bytes 1204232 | tf_op jit(solution)/shard_map/ppermute | solution.py:17
  238.0 31.2 %all-to-all-start = ((bf16[16,7,28,256]{3,2,1,0:T(8,128)(2,1)}), bf16[16,7,28,256]{3,2,1,0:T(8,128)(2,1)S(1)}, u32[]{:S(2)}, u32[]{:S(2)}) async-start(bf16[16,7,28,256]{3,2,1,0:T(8,128)(2,1)} %fusion.55), calls=%async_computation | async-start | bytes 3670016 | tf_op jit(solution)/shard_map/all_to_all | solution.py:249
  245.7 510.1 %all-reduce.4.cloned.1.call-start = ((), (), s32[]{:S(2)}) async-start(), calls=%async_computation.2 | async-start | bytes 10485760 | tf_op jit(solution)/shard_map/psum | solution.py:261
  295.7 30.8 %copy-start.10 = (bf16[16,7,28,256]{3,0,2,1:T(8,128)(2,1)S(1)}, bf16[16,7,28,256]{3,0,2,1:T(8,128)(2,1)}, u32[]{:S(2)}) copy-start(bf16[16,7,28,256]{3,0,2,1:T(8,128)(2,1)} %copy-done.9) | copy-start | bytes 4816900
  295.7 30.8 %copy-start.22 = (f32[16,7,28]{0,2,1:T(8,128)S(1)}, f32[16,7,28]{0,2,1:T(8,128)}, u32[]{:S(2)}) copy-start(f32[16,7,28]{0,2,1:T(8,128)} %copy-done.21) | copy-start | bytes 37636
  295.7 30.8 %copy-start.26 = (f32[16,7,28]{0,2,1:T(8,128)S(1)}, f32[16,7,28]{0,2,1:T(8,128)}, u32[]{:S(2)}) copy-start(f32[16,7,28]{0,2,1:T(8,128)} %copy-done.25) | copy-start | bytes 37636
  295.7 30.8 %copy-start.44 = (f32[256]{0:T(256)S(1)}, f32[256]{0:T(256)}, u32[]{:S(2)}) copy-start(f32[256]{0:T(256)} %param.17) | copy-start | bytes 3076
  324.1 10.5 %collective-permute-start.4 = (bf16[4,7,28,256]{3,0,2,1:T(4,128)(2,1)S(1)}, bf16[4,7,28,256]{3,0,2,1:T(4,128)(2,1)}, u32[]{:S(2)}, u32[]{:S(2)}) collective-permute-start(bf16[4,7,28,256]{3,0,2,1:T(4,128)(2,1)S(1)} %slice_bitcast_fusion), channel_id=1, source_target_pairs={{4,0},{8,4},{12,8},{16,12},{20,16},{24,20},{28,24},{32,28},{36,32}... | collective-permute-start | bytes 1204232 | tf_op jit(solution)/shard_map/ppermute | solution.py:17
  336.9 14.3 %collective-permute-start.5 = (bf16[16,3,28,256]{3,0,2,1:T(8,128)(2,1)}, bf16[16,3,28,256]{3,0,2,1:T(8,128)(2,1)}, u32[]{:S(2)}, u32[]{:S(2)}) collective-permute-start(bf16[16,3,28,256]{3,0,2,1:T(8,128)(2,1)} %copy.113), channel_id=1, source_target_pairs={{1,0},{2,1},{3,2},{0,3},{5,4},{6,5},{7,6},{4,7},{9,8},{10,9},{11,1... | collective-permute-start | bytes 2064392 | tf_op jit(solution)/shard_map/ppermute | solution.py:17
  408.0 26.8 %copy-start.6 = (bf16[4,392,256]{1,2,0:T(8,128)(2,1)S(1)}, bf16[4,392,256]{1,2,0:T(8,128)(2,1)}, u32[]{:S(2)}) copy-start(bf16[4,392,256]{1,2,0:T(8,128)(2,1)} %get-tuple-element.275) | copy-start | bytes 2408452 | tf_op jit(solution)/shard_map/while
  495.7 26.8 %copy-start.6 = (bf16[4,392,256]{1,2,0:T(8,128)(2,1)S(1)}, bf16[4,392,256]{1,2,0:T(8,128)(2,1)}, u32[]{:S(2)}) copy-start(bf16[4,392,256]{1,2,0:T(8,128)(2,1)} %get-tuple-element.275) | copy-start | bytes 2408452 | tf_op jit(solution)/shard_map/while
  600.5 13.7 %copy-start.15 = (f32[784,1024]{1,0:T(8,128)S(1)}, f32[784,1024]{1,0:T(8,128)}, u32[]{:S(2)}) copy-start(f32[784,1024]{1,0:T(8,128)} %reshape.292) | copy-start | bytes 9633796
  600.5 13.7 %copy-start.38 = (f32[784]{0:T(1024)S(1)}, f32[784]{0:T(1024)}, u32[]{:S(2)}) copy-start(f32[784]{0:T(1024)} %copy-done.37) | copy-start | bytes 9412
  600.5 13.7 %copy-start.40 = (f32[784]{0:T(1024)S(1)}, f32[784]{0:T(1024)}, u32[]{:S(2)}) copy-start(f32[784]{0:T(1024)} %copy-done.39) | copy-start | bytes 9412
  600.5 13.7 %copy-start.42 = (f32[1024]{0:T(1024)S(1)}, f32[1024]{0:T(1024)}, u32[]{:S(2)}) copy-start(f32[1024]{0:T(1024)} %param.23) | copy-start | bytes 12292
  600.5 12.7 %collective-permute-start.6 = (bf16[16,3,28,256]{3,0,2,1:T(8,128)(2,1)S(1)}, bf16[16,3,28,256]{3,0,2,1:T(8,128)(2,1)S(1)}, u32[]{:S(2)}, u32[]{:S(2)}) collective-permute-start(bf16[16,3,28,256]{3,0,2,1:T(8,128)(2,1)S(1)} %copy.120), channel_id=1, source_target_pairs={{3,0},{0,1},{1,2},{2,3},{7,4},{4,5},{5,6},{6,7},{11,8},{8,9},{9,10... | collective-permute-start | bytes 2064392 | tf_op jit(solution)/shard_map/ppermute | solution.py:17
  614.3 76.6 %collective-permute-start.7 = (bf16[4,7,28,256]{3,2,1,0:T(8,128)(2,1)}, bf16[4,7,28,256]{3,2,1,0:T(8,128)(2,1)S(1)}, u32[]{:S(2)}, u32[]{:S(2)}) collective-permute-start(bf16[4,7,28,256]{3,2,1,0:T(8,128)(2,1)} %pad_maximum_fusion.12), channel_id=1, source_target_pairs={{124,0},{0,4},{4,8},{8,12},{12,16},{16,20},{20,24},{24,28},{28,32}... | collective-permute-start | bytes 1204232 | tf_op jit(solution)/shard_map/ppermute | solution.py:17
  (44 other events, 238.6 us)
Sparse Core Ops, SparseCore 0:
  590.5 165.2 all-reduce.3
where the time goes:
time: 782 us; the launch traced here: 771 us
  matrix products  269 us (34%)
  local copies, waits for them, and re-layouts  170 us (22%)
  waiting for transfers between devices  132 us (17%)
  blocking collectives  94.3 us (12%)
  other arithmetic  68.1 us (9%)
  starting transfers between devices  21.6 us (3%)
  between operations  15 us (2%)
    psum x1, blocking collectives, local(): lax.psum((grad_qkv, grad_proj, grad_up, grad_down, grad_gain1, grad_gain2...  69.7 us
    psum x1, waiting for transfers between devices, local(): lax.psum((grad_qkv, grad_proj, grad_up, grad_down, grad_gain1, grad_gain2...  61.7 us
    dot_general x2, matrix products, attend_backward(): jnp.einsum('nhqk,nkhd->nqhd', grad_scores, key_vecs, preferred_element_ty...  53.7 us
    dot_general x2, matrix products, attend_backward(): jnp.einsum('nhqk,nqhd->nkhd', grad_scores, query_vecs, preferred_element_...  53.1 us
    ppermute x8, waiting for transfers between devices, shifted(): return lax.ppermute(block, axis, route)  51.3 us
    dot_general x1, matrix products, block_forward(): up_rows = jnp.dot(second_in, up_weight, preferred_element_type=jnp.float32)  32 us
    dynamic_update_slice x2, other arithmetic, block_forward(): attended, probs = lax.map(attend_group, (qkv_win, id_win))  31.8 us
    sub x2, matrix products, attend_forward(): expon = jnp.exp(scores - row_top)  30.6 us
  transfers between devices with their start and end apart: 10, of which 8 were waited for; matrix products, arithmetic and copies ran while one was open for 6% of the time, Pallas kernels for 0%

commit v1 on v0

v1 whole, which is shorter than its diff:
```python
import math

import jax
import jax.numpy as jnp
from jax import lax
from jax.experimental import pallas as pl
from jax.experimental.pallas import tpu as pltpu
from jax.sharding import PartitionSpec as P

HEADS = 8
HEAD = 32
NPOS = 392
C = 256
HID = 1024
C3 = 512
EPS = 1e-05
LOG2E = 1.4426950408889634
LN2 = 0.6931471805599453
SCALE = 1.0 / math.sqrt(HEAD)
FAR = 1e30
F32 = jnp.float32
BF16 = jnp.bfloat16
MIB = 1024 * 1024


def dot_nn(left, right):
    return lax.dot_general(left, right, (((1,), (0,)), ((), ())), preferred_element_type=F32)


def dot_nt(left, right):
    return lax.dot_general(left, right, (((1,), (1,)), ((), ())), preferred_element_type=F32)


def dot_tn(left, right):
    return lax.dot_general(left, right, (((0,), (0,)), ((), ())), preferred_element_type=F32)


def norm_forward(values):
    centre = jnp.mean(values, axis=-1, keepdims=True)
    centred = values - centre
    spread = jnp.mean(centred * centred, axis=-1, keepdims=True)
    inverse = lax.rsqrt(spread + EPS)
    return centred * inverse, inverse


def norm_backward(normed, inverse, gain, incoming):
    gated = incoming * gain
    first_mean = jnp.mean(gated, axis=-1, keepdims=True)
    second_mean = jnp.mean(gated * normed, axis=-1, keepdims=True)
    return inverse * (gated - first_mean - normed * second_mean)


def gelu_and_slope(up):
    size = jnp.abs(up)
    base = 1.0 + (0.3275911 * 0.7071067811865476) * size
    guess = pl.reciprocal(base, approx=True)
    t = guess * (2.0 - base * guess)
    bell = jnp.exp2((-0.5 * LOG2E) * (up * up))
    series = 0.5 * 1.061405429 * t - 0.5 * 1.453152027
    series = series * t + 0.5 * 1.421413741
    series = series * t - 0.5 * 0.284496736
    series = series * t + 0.5 * 0.254829592
    tail = series * t * bell
    cdf = jnp.where(up >= 0.0, 1.0 - tail, tail)
    return up * cdf, cdf + up * (bell * 0.3989422804014327)


MESH = pl.DeviceIdType.MESH
RUNS = ((3, 0, 7), (10, 7, 7), (17, 14, 7), (24, 21, 4), (0, 25, 3))


def runs_of(wc):
    return range(wc, wc + 1) if wc < 3 else range(3, 5)


class Place:
    def __init__(self):
        self.m, self.r = lax.axis_index("tm"), lax.axis_index("rows")
        self.n_tm = lax.axis_size("tm")
        self.odd = lax.rem(self.r, 2)
        self.edge = jnp.where(self.r == 0, 1, 0)

    def at(self, dm, dr):
        return (lax.rem(self.m + dm + self.n_tm, self.n_tm), lax.rem(self.r + dr + 4, 4))

    def across(self):
        return (self.m, 3 - self.r)

    def holder(self, k):
        r = lax.rem(self.r - k + 4, 4)
        return self.at(-self.edge, k), self.at(jnp.where(r == 0, 1, 0), -k)

    def owner(self, k):
        r = lax.rem(self.r + k, 4)
        return self.at(jnp.where(r == 0, 1, 0), k), self.at(-self.edge, -k)

    def greet(self, sources, extra):
        barrier = pltpu.get_barrier_semaphore()
        for dev in sources:
            pl.semaphore_signal(barrier, inc=1, device_id=dev, device_id_type=MESH)

        @pl.when(self.r == 0)
        def _():
            pl.semaphore_signal(barrier, inc=1, device_id=extra, device_id_type=MESH)
            pl.semaphore_wait(barrier, len(sources) + 1)

        @pl.when(self.r != 0)
        def _():
            pl.semaphore_wait(barrier, len(sources))


def remote(src, dst, sems, n, dev):
    return pltpu.make_async_remote_copy(
        src_ref=src, dst_ref=dst, send_sem=sems[0].at[n], recv_sem=sems[1].at[n],
        device_id=dev, device_id_type=MESH,
    )


def pack(quarters):
    padded = jnp.concatenate([quarters, jnp.zeros((3, 4, C), F32)], axis=0).reshape(13, 4, 4, C)
    return jnp.concatenate([padded[:, n] for n in range(4)], axis=1).astype(BF16)


def unpack(packed):
    wide = packed.astype(F32)
    parts = [wide[:, 4 * n : 4 * (n + 1)].reshape(13, 1, 4, C) for n in range(4)]
    return jnp.concatenate(parts, axis=1).reshape(52, 4, C)[0:49]


def mask_rows(ids, pos, tw, wc):
    lane = lax.broadcasted_iota(jnp.int32, (1, 28), 1)
    first = lane == 7 * wc
    here = (lane >= 7 * wc) & (lane < 7 * wc + 7)
    frames = ids[0, pl.ds(pl.multiple_of(8 * tw, 8), 8), :]
    rows = ids[:, pl.ds(pl.multiple_of(8 * tw, 8), 8), :]

    def count(bits, kept):
        kept_bits = jnp.where(kept, bits.astype(F32), 0.0)
        return jnp.sum(jnp.sum(kept_bits, axis=0, keepdims=True), axis=1, keepdims=True)

    past = [
        count((frames >> 2) & 1, first),
        count(jnp.concatenate([(rows[i, 0:1] >> 1) & 1 for i in range(7)], axis=0), first),
        count(frames[0:1] & 1, here),
    ]
    bits = [
        jnp.where(pos[n : n + 1] >= extent - past[n], 1.0, 0.0)
        for n, extent in enumerate((8.0, 7.0, 7.0))
    ]
    none = [jnp.zeros((10, NPOS), F32)]
    keys = jnp.concatenate([v for b in bits for v in (b, 1.0 - b)] + none, axis=0)
    queries = jnp.concatenate([v for b in bits for v in (1.0 - b, b)] + none, axis=0) * -FAR
    return keys.astype(BF16), queries.astype(BF16)


def forward_kernel(
    tokens, gm, ids, pos, qkv_w, proj, gain1, gain2, up_w, down_w,
    x_out, qkv_out, exp_out, inv_out, att_out, hid_out, act_out, slope_out, out_out, qkv_t,
    gm_in, edge_in,
    tok, x_now, pack_t, halo_t, edge_out, own_sem, row_out, row_in, t_out, t_in, gm_out_sem, gm_in_sem,
    gm_own, edge_out_sem, edge_in_sem,
):
    tw, wc = pl.program_id(0), pl.program_id(1)
    place = Place()
    row_sems, t_sems = (row_out, row_in), (t_out, t_in)
    gm_sems, edge_sems = (gm_out_sem, gm_in_sem), (edge_out_sem, edge_in_sem)

    def own_copies():
        return [
            pltpu.make_async_copy(
                tokens.at[3:7, a : a + n], tok.at[0:4, b : b + n], own_sem.at[at]
            )
            for at, (a, b, n) in enumerate(((3, 0, 25), (0, 25, 3)))
        ]

    def row_copy(at):
        a, b, n = RUNS[at]
        return remote(
            tokens.at[0:3, a : a + n], tok.at[4:7, b : b + n], row_sems, at, place.at(0, -1)
        )

    def t_copy():
        return remote(pack_t.at[wc], halo_t.at[wc], t_sems, wc, place.at(-1, 0))

    def gm_copy(k, part):
        dev, _ = place.holder(k)
        band = lax.rem(place.r + k, 4)
        first = lax.rem(4 * band + 1 - band // 2 + 2 * part, 14)
        slot = lax.rem(place.r + 3, 4)
        src, dst = gm.at[pl.ds(first, 2)], gm_in.at[slot, 2 * part : 2 * part + 2]
        return remote(src, dst, gm_sems, 2 * k + part, dev)

    def gm_local(part):
        band = place.r
        first = lax.rem(4 * band + 1 - band // 2 + 2 * part, 14)
        slot = lax.rem(place.r + 3, 4)
        return pltpu.make_async_copy(
            gm.at[pl.ds(first, 2)], gm_in.at[slot, 2 * part : 2 * part + 2], gm_own.at[part]
        )

    def edge_copy(half):
        return remote(edge_out.at[half], edge_in.at[half], edge_sems, half, place.across())

    @pl.when((tw == 0) & (wc == 0))
    def _():
        for copy in own_copies():
            copy.start()
        sources = [place.at(0, 1), place.at(1, 0), place.across()]
        place.greet(sources + [place.holder(k)[1] for k in (1, 2, 3)], place.holder(0)[1])
        for at in range(5):
            row_copy(at).start()
        qkv_t[...] = qkv_w[...].astype(F32).T.astype(BF16)
        for copy in own_copies():
            copy.wait()

    @pl.when((tw == 0) & (wc == 1))
    def _():
        for k in (1, 2, 3):
            for part in range(2):
                gm_copy(k, part).start()

        @pl.when(place.r == 0)
        def _():
            for part in range(2):
                gm_copy(0, part).start()

        @pl.when(place.r != 0)
        def _():
            for part in range(2):
                gm_local(part).start()

    for window in range(4):

        @pl.when((tw == 0) & (wc == window))
        def _(window=window):
            for at in runs_of(window):
                row_copy(at).wait_recv()

    @pl.when(tw == 0)
    def _():
        block = tok[:, pl.ds(7 * wc, 7)].astype(F32).reshape(49, 16, C)
        pack_t[wc] = pack(block[:, 0:4])
        t_copy().start()
        x_now[...] = block[:, 4:12]

    @pl.when(tw == 1)
    def _():
        t_copy().wait_recv()
        block = tok[:, pl.ds(7 * wc, 7)].astype(F32).reshape(49, 16, C)
        x_now[...] = jnp.concatenate([block[:, 12:16], unpack(halo_t[wc])], axis=1)

    x = x_now[...].reshape(NPOS, C)
    x_out[0] = x.astype(BF16)
    mask_k, mask_q = mask_rows(ids, pos, tw, wc)
    normed, _ = norm_forward(x)
    first_in = (normed * gain1[...]).astype(BF16)
    rows = dot_nt(qkv_t[...], first_in)
    qkv_out[0, 0:C] = (rows[0:C] * (SCALE * LOG2E)).astype(BF16)
    qkv_out[0, C:] = rows[C:].astype(BF16)
    for h in range(HEADS):
        here = slice(HEAD * h, HEAD * (h + 1))
        q = jnp.concatenate([qkv_out[0, HEAD * h : HEAD * (h + 1)], mask_q], axis=0)
        k = jnp.concatenate([qkv_out[0, C + HEAD * h : C + HEAD * (h + 1)], mask_k], axis=0)
        v = qkv_out[0, 2 * C + HEAD * h : 2 * C + HEAD * (h + 1)]
        scores = dot_tn(k, q)
        top = jnp.max(scores, axis=0, keepdims=True)
        expon = jnp.exp2(scores - top)
        inverse = 1.0 / jnp.sum(expon, axis=0, keepdims=True)
        expon = expon.astype(BF16)
        exp_out[0, h] = expon
        inv_out[0, h : h + 1] = inverse
        att_out[0, here] = (dot_nn(v, expon) * inverse).astype(BF16)
    hidden = (x + dot_tn(att_out[0], proj[...])).astype(BF16)
    hid_out[0] = hidden
    hidden = hidden.astype(F32)
    normed, _ = norm_forward(hidden)
    second_in = (normed * gain2[...]).astype(BF16)
    result = hidden
    for part in range(4):
        cols = slice(256 * part, 256 * (part + 1))
        act, slope = gelu_and_slope(dot_nn(second_in, up_w[:, cols]))
        act = act.astype(BF16)
        act_out[0, :, cols] = act
        slope_out[0, :, cols] = slope.astype(BF16)
        result = result + dot_nn(act, down_w[cols])
    out_out[0] = result.astype(BF16)
    edge = jnp.where(place.odd == 1, result[336:392], result[0:56])
    edge_out[tw, wc] = edge.astype(BF16)

    @pl.when((tw == 0) & (wc == 3))
    def _():
        edge_copy(0).start()

    @pl.when((tw == 1) & (wc == 3))
    def _():
        edge_copy(1).start()
        for at in range(5):
            row_copy(at).wait_send()
        for n in range(4):
            remote(pack_t.at[n], halo_t.at[n], t_sems, n, place.at(-1, 0)).wait_send()
        for k in (1, 2, 3):
            for part in range(2):
                gm_copy(k, part).wait()

        @pl.when(place.r == 0)
        def _():
            for part in range(2):
                gm_copy(0, part).wait()

        @pl.when(place.r != 0)
        def _():
            for part in range(2):
                gm_local(part).wait()

        for half in range(2):
            edge_copy(half).wait()


def whole(shape):
    return pl.BlockSpec(shape, lambda *_: (0,) * len(shape))


def by_window(shape, backwards=False):
    def index(tw, wc):
        return (4 * (1 - tw if backwards else tw) + wc,) + (0,) * len(shape)

    return pl.BlockSpec((1,) + shape, index)


SMEM_SPEC = pl.BlockSpec(memory_space=pltpu.SMEM)
ANY_SPEC = pl.BlockSpec(memory_space=pl.ANY)
DMA = pltpu.SemaphoreType.DMA


def positions():
    at = jnp.arange(NPOS)
    rows = [at % 8, at // 56, (at // 8) % 7]
    return jnp.concatenate([jnp.stack(rows), jnp.zeros((5, NPOS), at.dtype)]).astype(F32)


def run_forward(tokens, gm, ids, qkv_w, proj, gain1, gain2, up_w, down_w):
    saved = [
        ((NPOS, C), BF16),
        ((3 * C, NPOS), BF16),
        ((HEADS, NPOS, NPOS), BF16),
        ((HEADS, NPOS), F32),
        ((C, NPOS), BF16),
        ((NPOS, C), BF16),
        ((NPOS, HID), BF16),
        ((NPOS, HID), BF16),
        ((NPOS, C), BF16),
    ]
    pos = positions()
    return pl.pallas_call(
        forward_kernel,
        grid=(2, 4),
        out_shape=[jax.ShapeDtypeStruct((8,) + shape, kind) for shape, kind in saved]
        + [
            jax.ShapeDtypeStruct((3 * C, C), BF16),
            jax.ShapeDtypeStruct((4, 4, 14, 4, C3), BF16),
            jax.ShapeDtypeStruct((2, 4, 56, C), BF16),
        ],
        in_specs=[ANY_SPEC, ANY_SPEC, whole(ids.shape), whole(pos.shape)]
        + [whole(w.shape) for w in (qkv_w, proj, gain1, gain2, up_w, down_w)],
        out_specs=[by_window(shape) for shape, _ in saved]
        + [whole((3 * C, C)), ANY_SPEC, ANY_SPEC],
        scratch_shapes=[
            pltpu.VMEM((7, 28, 16, C), BF16),
            pltpu.VMEM((49, 8, C), F32),
            pltpu.VMEM((4, 13, 16, C), BF16),
            pltpu.VMEM((4, 13, 16, C), BF16),
            pltpu.VMEM((2, 4, 56, C), BF16),
            DMA((2,)), DMA((5,)), DMA((5,)), DMA((4,)), DMA((4,)), DMA((8,)), DMA((8,)),
            DMA((2,)), DMA((2,)), DMA((2,)),
        ],
        compiler_params=pltpu.CompilerParams(
            vmem_limit_bytes=58 * MIB, collective_id=1, has_side_effects=True
        ),
        name="forward",
    )(tokens, gm, ids, pos, qkv_w, proj, gain1, gain2, up_w, down_w)


def to_blocks(blocks, first, values):
    height, width = values.shape
    for a in range(height // 256):
        for b in range(width // 128):
            part = values[256 * a : 256 * (a + 1), 128 * b : 128 * (b + 1)]
            blocks[first + a * (width // 128) + b] = part.astype(BF16)


def from_blocks(blocks, first, height, width):
    rows, cols = height // 256, width // 128
    part = blocks[first : first + rows * cols].reshape(rows, cols, 256, 128)
    return part.transpose(0, 2, 1, 3).reshape(height, width).astype(F32)


def column_runs(wc):
    if wc < 3:
        return [(7 * wc + 3, 0, 7)]
    return [(24, 0, 4), (0, 4, 7)]


def merge_kernel(
    out_win, edge, gm, gain3, reduce_w, place,
    grad_out, m_all, reduce_blocks, grad_gain,
    rows, third_all, gm_rows, grad_reduce,
):
    tw = pl.program_id(0)
    r = place[0]
    odd = lax.rem(r, 2)

    @pl.when(tw == 0)
    def _():
        grad_reduce[...] = jnp.zeros_like(grad_reduce)
        grad_gain[...] = jnp.zeros_like(grad_gain)

    for wc in range(4):
        block = out_win[wc].astype(F32).reshape(7, 7, 8, C)
        strip = edge[0, wc].astype(F32).reshape(7, 8, C)
        for start, first, last in column_runs(wc):
            cols = slice(start, start + last - first)
            rows[pl.ds(1 - odd, 7), cols] = block[:, first:last]
            rows[7 * odd, cols] = strip[first:last]

    gain = gain3[...]
    for a in range(4):
        upper = rows[2 * a].reshape(14, 2, 8, C)
        lower = rows[2 * a + 1].reshape(14, 2, 8, C)
        joined = jnp.concatenate(
            [upper[:, 0], lower[:, 0], upper[:, 1], lower[:, 1]], axis=-1
        ).reshape(112, 4 * C)
        normed, inverse = norm_forward(joined)
        third = normed * gain
        merged = dot_nn(third.astype(BF16), reduce_w[...])
        merged = merged.reshape(14, 8, C3)
        m_all[0, a] = merged[:, 0:4].astype(BF16)
        m_all[1, a] = merged[:, 4:8].astype(BF16)
        grads = jnp.concatenate([gm[0, a].astype(F32), gm[1, a].astype(F32)], axis=1)
        grads = grads.reshape(112, C3).astype(BF16)
        gz = dot_nt(grads, reduce_w[...])
        gz_sum = jnp.sum(gz * normed, axis=0, keepdims=True)
        if a == 0:
            counted = jnp.where((odd == 0) & (tw == 1), 0.0, 1.0)
        elif a == 3:
            counted = jnp.where((odd == 1) & (tw == 0), 0.0, 1.0)
        else:
            counted = None
        if counted is not None:
            third = third * counted
            gz_sum = gz_sum * counted
        grad_gain[...] += gz_sum
        third_all[112 * a : 112 * (a + 1)] = third.astype(BF16)
        gm_rows[112 * a : 112 * (a + 1)] = grads
        back = norm_backward(normed, inverse, gain, gz).reshape(14, 8, 4 * C)
        pieces = [back[:, :, C * n : C * (n + 1)].reshape(14, 1, 8, C) for n in range(4)]
        rows[2 * a] = jnp.concatenate([pieces[0], pieces[2]], axis=1).reshape(28, 8, C)
        rows[2 * a + 1] = jnp.concatenate([pieces[1], pieces[3]], axis=1).reshape(28, 8, C)
    grad_reduce[...] += dot_tn(third_all[...], gm_rows[...])
    for wc in range(4):
        runs = [
            rows[pl.ds(1 - odd, 7), start : start + last - first]
            for start, first, last in column_runs(wc)
        ]
        block = runs[0] if len(runs) == 1 else jnp.concatenate(runs, axis=1)
        grad_out[wc] = block.reshape(NPOS, C).astype(BF16)

    @pl.when(tw == 1)
    def _():
        to_blocks(reduce_blocks, 0, grad_reduce)


def run_merge(out_win, edge, gm, gain3, reduce_w, place):
    def by_tw(shape):
        return pl.BlockSpec(shape, lambda tw: (tw,) + (0,) * (len(shape) - 1))

    pieces = (2, 4, 14, 4, C3)
    return pl.pallas_call(
        merge_kernel,
        grid=(2,),
        out_shape=[
            jax.ShapeDtypeStruct((8, NPOS, C), BF16),
            jax.ShapeDtypeStruct((4, 4, 14, 4, C3), BF16),
            jax.ShapeDtypeStruct((16, 256, 128), BF16),
            jax.ShapeDtypeStruct((1, 4 * C), F32),
        ],
        in_specs=[by_tw((4, NPOS, C)), by_tw((1, 4, 56, C)), by_tw(pieces)]
        + [whole((1, 4 * C)), whole((4 * C, C3)), SMEM_SPEC],
        out_specs=[by_tw((4, NPOS, C)), by_tw(pieces), whole((16, 256, 128)), whole((1, 4 * C))],
        scratch_shapes=[
            pltpu.VMEM((8, 28, 8, C), F32),
            pltpu.VMEM((448, 4 * C), BF16),
            pltpu.VMEM((448, C3), BF16),
            pltpu.VMEM((4 * C, C3), F32),
        ],
        compiler_params=pltpu.CompilerParams(vmem_limit_bytes=58 * MIB),
        name="merge",
    )(out_win, edge, gm, gain3, reduce_w, place)


def backward_kernel(
    grad_out, x_in, qkv_in, exp_in, inv_in, att_in, hid_in, act_in, slope_in,
    qkv_t, proj, gain1, gain2, up_w, down_w, reduce_blocks, grad_gain3, pieces,
    blocks, merged, grad_tokens,
    grad_rows_t, grad_qkv_t, grad_proj, grad_up, grad_down_t, grad_gain1, grad_gain2,
    late, final, pack_t, halo_t, t_out, t_in, row_out, row_in, own_sem, m_out, m_in, m_own,
):
    tw, wc = 1 - pl.program_id(0), pl.program_id(1)
    place = Place()
    t_sems, row_sems, m_sems = (t_out, t_in), (row_out, row_in), (m_out, m_in)

    def m_ends(k, n):
        c = lax.rem(place.r + k + 3, 4)
        start = 4 * place.r + 1 - place.r // 2
        first = (1 - place.odd, 3 - place.odd, 3)[n]
        count = (2, 1, 1)[n]
        return (
            pieces.at[c, pl.ds(first, count)],
            merged.at[pl.ds(lax.rem(start + first, 14), count)],
        )

    def m_copy(k, n):
        return remote(*m_ends(k, n), m_sems, 3 * k + n, place.owner(k)[0])

    def m_local(n):
        return pltpu.make_async_copy(*m_ends(0, n), m_own.at[n])

    def m_each(act_remote, act_local):
        for k in (1, 2, 3):
            act_remote(k, 0)
            act_remote(k, 1)

        @pl.when(place.r == 0)
        def _():
            act_remote(0, 0)
            act_remote(0, 1)

        @pl.when(place.r != 0)
        def _():
            act_local(0)
            act_local(1)

    def t_copy(n):
        return remote(pack_t.at[n], halo_t.at[n], t_sems, n, place.at(1, 0))

    def row_copy(at):
        a, b, n = RUNS[at]
        window, first = (at, 0) if at < 3 else (3, b - 21)
        return remote(
            final.at[window, 4:7, first : first + n], grad_tokens.at[0:3, a : a + n],
            row_sems, at, place.at(0, 1),
        )

    def own_copy(at):
        a, b, n = RUNS[at]
        window, first = (at, 0) if at < 3 else (3, b - 21)
        return pltpu.make_async_copy(
            final.at[window, 0:4, first : first + n], grad_tokens.at[3:7, a : a + n], own_sem.at[at]
        )

    @pl.when((tw == 1) & (wc == 0))
    def _():
        sources = [place.at(0, -1), place.at(-1, 0)]
        place.greet(sources + [place.owner(k)[1] for k in (1, 2, 3)], place.owner(0)[1])
        m_each(lambda k, n: m_copy(k, n).start(), lambda n: m_local(n).start())

        @pl.when(place.odd == 1)
        def _():
            for k in (1, 2, 3):
                m_copy(k, 2).start()
            m_local(2).start()

        for ref in (grad_qkv_t, grad_proj, grad_up, grad_down_t, grad_gain1, grad_gain2):
            ref[...] = jnp.zeros_like(ref)

    grad_rows = grad_out[0]
    normed2, inverse2 = norm_forward(hid_in[0].astype(F32))
    second_in = (normed2 * gain2[...]).astype(BF16)
    grad_second = jnp.zeros((NPOS, C), F32)
    for part in range(4):
        cols = slice(256 * part, 256 * (part + 1))
        grad_down_t[:, cols] += dot_tn(grad_rows, act_in[0, :, cols])
        grad_act = dot_nt(grad_rows, down_w[cols])
        grad_up_in = (grad_act * slope_in[0, :, cols].astype(F32)).astype(BF16)
        grad_up[:, cols] += dot_tn(second_in, grad_up_in)
        grad_second = grad_second + dot_nt(grad_up_in, up_w[:, cols])
    grad_gain2[...] += jnp.sum(grad_second * normed2, axis=0, keepdims=True)
    grad_hidden = grad_rows.astype(F32) + norm_backward(normed2, inverse2, gain2[...], grad_second)
    grad_hidden_b = grad_hidden.astype(BF16)
    grad_proj[...] += dot_nn(att_in[0], grad_hidden_b)
    grad_att = dot_nt(proj[...], grad_hidden_b).astype(BF16)
    for h in range(HEADS):
        at_q = slice(HEAD * h, HEAD * (h + 1))
        at_k = slice(C + HEAD * h, C + HEAD * (h + 1))
        at_v = slice(2 * C + HEAD * h, 2 * C + HEAD * (h + 1))
        expon = exp_in[0, h]
        incoming = (grad_att[at_q].astype(F32) * inv_in[0, h : h + 1]).astype(BF16)
        inner = jnp.sum(incoming.astype(F32) * att_in[0, at_q].astype(F32), axis=0, keepdims=True)
        grad_probs = dot_tn(qkv_in[0, at_v], incoming)
        grad_scores = (expon.astype(F32) * (grad_probs - inner)).astype(BF16)
        grad_rows_t[at_q] = (dot_nn(qkv_in[0, at_k], grad_scores) * SCALE).astype(BF16)
        grad_rows_t[at_k] = (dot_nt(qkv_in[0, at_q], grad_scores) * LN2).astype(BF16)
        grad_rows_t[at_v] = dot_nt(incoming, expon).astype(BF16)
    normed1, inverse1 = norm_forward(x_in[0].astype(F32))
    first_in = (normed1 * gain1[...]).astype(BF16)
    grad_qkv_t[...] += dot_nn(grad_rows_t[...], first_in)
    grad_first = dot_tn(grad_rows_t[...], qkv_t[...])
    grad_gain1[...] += jnp.sum(grad_first * normed1, axis=0, keepdims=True)
    grad_x = grad_hidden + norm_backward(normed1, inverse1, gain1[...], grad_first)
    block = grad_x.reshape(49, 8, C)

    @pl.when(tw == 1)
    def _():
        late[wc] = block[:, 0:4].astype(BF16)
        pack_t[wc] = pack(block[:, 4:8])
        t_copy(wc).start()

    @pl.when(tw == 0)
    def _():
        t_copy(wc).wait_recv()
        frames = jnp.concatenate([unpack(halo_t[wc]), block, late[wc].astype(F32)], axis=1)
        final[wc] = frames.astype(BF16).reshape(7, 7, 16, C)

    for window in range(4):

        @pl.when((tw == 0) & (wc == window))
        def _(window=window):
            for at in runs_of(window):
                row_copy(at).start()
                own_copy(at).start()

    @pl.when((tw == 0) & (wc == 3))
    def _():
        blocks[0:16] = reduce_blocks[...]
        to_blocks(blocks, 16, grad_up)
        to_blocks(blocks, 24, grad_down_t[...].T)
        to_blocks(blocks, 32, grad_qkv_t[...].T)
        to_blocks(blocks, 38, grad_proj)
        gains = [grad_gain1, grad_gain1, grad_gain2, grad_gain2] + [grad_gain3] * 8
        lanes = [0, 1, 0, 1] + list(range(8))
        rows = [ref[:, 128 * n : 128 * (n + 1)] for ref, n in zip(gains, lanes)]
        blocks[40, 0:16] = jnp.concatenate(rows + [jnp.zeros((4, 128), F32)], axis=0).astype(BF16)
        blocks[40, 16:256] = jnp.zeros((240, 128), BF16)
        blocks[41:48] = jnp.zeros((7, 256, 128), BF16)
        for at in range(5):
            row_copy(at).wait()
            own_copy(at).wait()
        for n in range(4):
            t_copy(n).wait_send()
        m_each(lambda k, n: m_copy(k, n).wait(), lambda n: m_local(n).wait())

        @pl.when(place.odd == 1)
        def _():
            for k in (1, 2, 3):
                m_copy(k, 2).wait_send()
            m_local(2).wait()
            m_copy(2, 2).wait_recv()

        @pl.when(place.odd == 0)
        def _():
            for k in (1, 3):
                m_copy(k, 2).wait_recv()


def run_backward(grad_out, saved, *weights):
    sums = [(3 * C, C), (C, C), (C, HID), (C, HID), (1, C), (1, C)]
    *vmem_weights, _ = weights
    return pl.pallas_call(
        backward_kernel,
        grid=(2, 4),
        out_shape=[
            jax.ShapeDtypeStruct((48, 256, 128), BF16),
            jax.ShapeDtypeStruct((14, 14, 4, C3), BF16),
            jax.ShapeDtypeStruct((7, 28, 16, C), BF16),
        ],
        in_specs=[by_window(array.shape[1:], True) for array in (grad_out, *saved)]
        + [whole(w.shape) for w in vmem_weights]
        + [ANY_SPEC],
        out_specs=[whole((48, 256, 128)), ANY_SPEC, ANY_SPEC],
        scratch_shapes=[pltpu.VMEM((3 * C, NPOS), BF16)]
        + [pltpu.VMEM(shape, F32) for shape in sums]
        + [
            pltpu.VMEM((4, 49, 4, C), BF16),
            pltpu.VMEM((4, 7, 7, 16, C), BF16),
            pltpu.VMEM((4, 13, 16, C), BF16),
            pltpu.VMEM((4, 13, 16, C), BF16),
            DMA((4,)), DMA((4,)), DMA((5,)), DMA((5,)), DMA((5,)), DMA((12,)), DMA((12,)), DMA((3,)),
        ],
        compiler_params=pltpu.CompilerParams(
            vmem_limit_bytes=58 * MIB, collective_id=2, has_side_effects=True
        ),
        name="backward",
    )(grad_out, *saved, *weights)


ORDERS = (("x", "y", "z"), ("y", "z", "x"), ("z", "x", "y"))
PART = 2048


def torus(n_tm):
    return {32: (4, 2, 4), 8: (2, 2, 2), 4: (1, 2, 2), 2: (1, 2, 1)}[n_tm]


class Torus:
    def __init__(self, dims):
        self.dims = dims
        _, n_yl, n_z = dims
        m, r = lax.axis_index("tm"), lax.axis_index("rows")
        self.core = lax.rem(r, 2)
        self.sizes = {"x": dims[0], "y": 2 * n_yl, "z": n_z}
        self.at = {
            "x": m // (n_yl * n_z),
            "y": (r // 2) * n_yl + lax.rem(m // n_z, n_yl),
            "z": lax.rem(m, n_z),
        }

    def device(self, core=None, **moved):
        _, n_yl, n_z = self.dims
        at = {**self.at, **moved}
        core = self.core if core is None else core
        m = (at["x"] * n_yl + lax.rem(at["y"], n_yl)) * n_z + at["z"]
        return (m, (at["y"] // n_yl) * 2 + core)

    def partners(self, axis):
        size = self.sizes[axis]
        places = [lax.rem(self.at[axis] + j, size) for j in range(1, size)]
        return [(place, self.device(**{axis: place})) for place in places]


def sum_kernel(dims, blocks, total, core_in, acc0, acc1, acc2, in1, in2, in3, *sems):
    core_send, core_recv, rs_send, rs_recv, ag_send, ag_recv, back_send, back_recv = sems
    here = Torus(dims)
    other = here.device(core=1 - here.core)
    everyone = [other] + [dev for axis in "xyz" for _, dev in here.partners(axis)]
    barrier = pltpu.get_barrier_semaphore()
    for dev in everyone:
        pl.semaphore_signal(barrier, inc=1, device_id=dev, device_id_type=pl.DeviceIdType.MESH)
    pl.semaphore_wait(barrier, len(everyone))

    def send(src, dst, out_sem, in_sem, dev):
        copy = pltpu.make_async_remote_copy(
            src_ref=src, dst_ref=dst, send_sem=out_sem, recv_sem=in_sem,
            device_id=dev, device_id_type=pl.DeviceIdType.MESH,
        )
        copy.start()
        return copy

    def rows(start, length):
        return pl.ds(pl.multiple_of(start, length), length)

    mine = here.core * (3 * PART)
    theirs = (1 - here.core) * (3 * PART)
    copies = [
        send(
            blocks.at[rows(theirs + p * PART, PART)], core_in.at[p],
            core_send.at[p], core_recv.at[p], other,
        )
        for p in range(3)
    ]
    finished = list(copies)
    accs, ins = (acc0, acc1, acc2), (in1, in2, in3)
    in_flight = [[copy] for copy in copies]
    starts = [mine + p * PART for p in range(3)]
    lengths = [PART] * 3
    regions = [[] for _ in range(3)]
    for s in range(4):
        for p in range(3):
            for copy in in_flight[p]:
                copy.wait_recv()
            if s == 0:
                value = blocks[rows(starts[p], PART)].astype(F32) + core_in[p].astype(F32)
            else:
                axis = ORDERS[p][s - 1]
                place, length = here.at[axis], lengths[p] // here.sizes[axis]
                value = accs[s - 1][p, rows(place * length, length)].astype(F32)
                for j in range(here.sizes[axis] - 1):
                    value = value + ins[s - 1][p, j].astype(F32)
                starts[p] = starts[p] + place * length
                lengths[p] = length
            regions[p].append((starts[p], lengths[p]))
            if s == 3:
                total[rows(starts[p], lengths[p])] = value.astype(BF16)
                continue
            accs[s][p] = value.astype(BF16)
            axis = ORDERS[p][s]
            length = lengths[p] // here.sizes[axis]
            in_flight[p] = [
                send(
                    accs[s].at[p, rows(place * length, length)], ins[s].at[p, j],
                    rs_send.at[s, p, j], rs_recv.at[s, p, j], dev,
                )
                for j, (place, dev) in enumerate(here.partners(axis))
            ]
            finished += in_flight[p]

    in_flight = [[], [], []]
    for s in (3, 2, 1, 0):
        for p in range(3):
            for copy in in_flight[p]:
                copy.wait_recv()
            region = total.at[rows(*regions[p][s])]
            if s == 0:
                in_flight[p] = [send(region, region, back_send.at[p], back_recv.at[p], other)]
            else:
                in_flight[p] = [
                    send(region, region, ag_send.at[s - 1, p, j], ag_recv.at[s - 1, p, j], dev)
                    for j, (_, dev) in enumerate(here.partners(ORDERS[p][s - 1]))
                ]
            finished += in_flight[p]
    for p in range(3):
        for copy in in_flight[p]:
            copy.wait_recv()
    for copy in finished:
        copy.wait_send()


def run_sum(blocks, n_tm):
    dims = torus(n_tm)
    sizes = (dims[0], 2 * dims[1], dims[2])
    assert min(sizes) == max(sizes) or n_tm != 32
    lengths, ins = [PART], []
    if min(sizes) == max(sizes):
        for size in sizes:
            lengths.append(lengths[-1] // size)
            ins.append((3, size - 1, lengths[-1], 128))
    sem = pltpu.SemaphoreType.DMA
    most = max(sizes) - 1
    return pl.pallas_call(
        lambda *refs: sum_kernel(dims, *refs),
        out_shape=jax.ShapeDtypeStruct((6 * PART, 128), BF16),
        in_specs=[pl.BlockSpec(memory_space=pltpu.VMEM)],
        out_specs=pl.BlockSpec(memory_space=pltpu.VMEM),
        scratch_shapes=[pltpu.VMEM((3, PART, 128), BF16)]
        + [pltpu.VMEM((3, length, 128), BF16) for length in lengths[:3]]
        + [pltpu.VMEM(shape, BF16) for shape in ins]
        + [sem((3,)), sem((3,)), sem((3, 3, most)), sem((3, 3, most)), sem((3, 3, most)), sem((3, 3, most))]
        + [sem((3,)), sem((3,))],
        compiler_params=pltpu.CompilerParams(
            collective_id=0, has_side_effects=True, vmem_limit_bytes=32 * MIB
        ),
        name="sum_all",
    )(blocks.reshape(6 * PART, 128)).reshape(48, 256, 128)


def spread_kernel(blocks, qkv, proj, up, down, reduce_w, gains):
    for ref, first in ((qkv, 32), (proj, 38), (up, 16), (down, 24), (reduce_w, 0)):
        height, width = ref.shape
        for a in range(height // 256):
            for b in range(width // 128):
                part = blocks[first + a * (width // 128) + b].astype(F32)
                ref[256 * a : 256 * (a + 1), 128 * b : 128 * (b + 1)] = part
    gains[...] = blocks[40, 0:16].astype(F32)


def run_spread(blocks):
    shapes = [(C, 3 * C), (C, C), (C, HID), (HID, C), (4 * C, C3), (16, 128)]
    return pl.pallas_call(
        spread_kernel,
        out_shape=[jax.ShapeDtypeStruct(shape, F32) for shape in shapes],
        compiler_params=pltpu.CompilerParams(vmem_limit_bytes=32 * MIB),
        name="spread",
    )(blocks)


def local(
    tokens, region_ids, gain_attn, qkv_weight, proj_weight, gain_mlp, up_weight, down_weight,
    gain_merge, reduce_weight, grad_merged,
):
    n_tm = lax.axis_size("tm")
    place = lax.axis_index("rows").astype(jnp.int32).reshape(1)
    gain1, gain2, gain3 = (g.reshape(1, -1) for g in (gain_attn, gain_mlp, gain_merge))
    *saved, out_win, qkv_t, gm, edge = run_forward(
        tokens.transpose(1, 2, 0, 3), grad_merged.transpose(1, 2, 0, 3),
        region_ids.transpose(1, 0, 2), qkv_weight, proj_weight, gain1, gain2, up_weight, down_weight,
    )
    grad_out, pieces, grad_reduce, grad_gain3 = run_merge(
        out_win, edge, gm, gain3, reduce_weight, place
    )
    blocks, merged, grad_tokens = run_backward(
        grad_out, saved, qkv_t, proj_weight, gain1, gain2, up_weight, down_weight, grad_reduce,
        grad_gain3, pieces,
    )
    *grads, gains = run_spread(run_sum(blocks, n_tm))
    gains = gains.reshape(-1)
    return (
        merged.transpose(2, 0, 1, 3),
        grad_tokens.transpose(2, 0, 1, 3),
        *grads,
        gains[0:256],
        gains[256:512],
        gains[512:1536],
    )


def solution(mesh):
    placed = (
        P("tm", "rows", None, None),
        P("tm", "rows", None),
        P(), P(), P(), P(), P(), P(), P(), P(),
        P(("tm", "rows"), None, None, None),
    )
    return jax.shard_map(
        local,
        mesh=mesh,
        in_specs=placed,
        out_specs=(
            P(("tm", "rows"), None, None, None),
            P("tm", "rows", None, None),
            P(), P(), P(), P(), P(), P(), P(), P(),
        ),
        check_vma=False,
    )
```

time: 782 us -> 198 us (0.25); the launches traced: 771 us -> 198 us
  matrix products: 269 us -> 0 us
  Pallas kernels: 0 us -> 191 us
  local copies, waits for them, and re-layouts: 170 us -> 5.17 us
  waiting for transfers between devices: 132 us -> 0 us
  blocking collectives: 94.3 us -> 0 us
  other arithmetic: 68.1 us -> 0.7 us
  starting transfers between devices: 21.6 us -> 0 us
  between operations: 15 us -> 0.71 us
    dot_general x25 -> x0, matrix products: 239 us -> none  [the longest x2 53.7 us: attend_backward(): jnp.einsum('nhqk,nkhd->nqhd', grad_scores, key_vecs, preferred_element_ty...]
    pallas_call x0 -> x5, Pallas kernels: none -> 191 us  [the longest x1 68.5 us: run_backward(): pl.pallas_call(backward_kernel, grid=(2, 4), out_shape=[jax.ShapeDtypeStr...]
    psum x1 -> x0, blocking collectives: 69.7 us -> none  [local(): lax.psum((grad_qkv, grad_proj, grad_up, grad_down, grad_gain1, grad_gain2...]
    psum x1 -> x0, waiting for transfers between devices: 61.7 us -> none  [local(): lax.psum((grad_qkv, grad_proj, grad_up, grad_down, grad_gain1, grad_gain2...]
    ppermute x8 -> x0, waiting for transfers between devices: 51.3 us -> none  [shifted(): return lax.ppermute(block, axis, route)]
    dynamic_update_slice x2 -> x0, other arithmetic: 31.8 us -> none  [block_forward(): attended, probs = lax.map(attend_group, (qkv_win, id_win))]
    sub x2 -> x0, matrix products: 30.6 us -> none  [attend_forward(): expon = jnp.exp(scores - row_top)]
    convert_element_type x9 -> x0, local copies, waits for them, and re-layouts: 27.7 us -> none  [the longest x3 11.3 us: merge_both(): normed3, inverse3 = norm_forward(joined.astype(jnp.float32))]
  transfers between devices with their start and end apart: 10 -> 0, of which waited for: 8 -> 0; matrix products, arithmetic and copies ran while one was open for 6% -> 0% of each run, Pallas kernels for 0% -> 0%
where the time goes in v1:
time: 198 us
  Pallas kernels  191 us (96%)
  local copies, waits for them, and re-layouts  5.17 us (3%)
    pallas_call x1, Pallas kernels, run_backward(): pl.pallas_call(backward_kernel, grid=(2, 4), out_shape=[jax.ShapeDtypeStr...  68.5 us
    pallas_call x1, Pallas kernels, run_forward(): pl.pallas_call(forward_kernel, grid=(2, 4), out_shape=[jax.ShapeDtypeStru...  68.5 us
    pallas_call x1, Pallas kernels, run_sum(): pl.pallas_call(lambda *refs: sum_kernel(dims, *refs), out_shape=jax.Shape...  41.4 us
    pallas_call x1, Pallas kernels, run_merge(): pl.pallas_call(merge_kernel, grid=(2,), out_shape=[jax.ShapeDtypeStruct((...  10.3 us

profile of v1, /device:TPU:1, one launch (start us, length us, event | category | flops | bytes accessed | tf_op | source)
XLA Modules:
  0.0 198.0 jit_solution(3023355630582185860)
XLA Ops:
  0.7 0.1 pad.3.clone
  0.8 0.7 add_convert_fusion.pos
  1.4 68.5 %forward.1 = (bf16[8,392,256]{2,1,0:T(8,128)(2,1)}, bf16[8,768,392]{2,1,0:T(8,128)(2,1)}, bf16[8,8,392,392]{3,2,1,0:T(8,128)(2,1)}, f32[8,8,392]{2,1,0:T(8,128)}...) custom-call(bf16[7,28,16,256]{3,2,1,0:T(8,128)(2,1)} %bitcast.19, ...), custom_call_target="tpu_custom_call" | custom-call | tf_op jit(solution)/shard_map/forward/pallas_call | solution.py:354
  70.0 10.3 %merge.1 = (bf16[8,392,256]{2,1,0:T(8,128)(2,1)}, bf16[4,4,14,4,512]{4,3,2,1,0:T(4,128)(2,1)}, bf16[16,256,128]{2,1,0:T(8,128)(2,1)}, f32[1,1024]{1,0:T(1,128)}) custom-call(bf16[8,392,256]{2,1,0:T(8,128)(2,1)} %get-tuple-element.35.out_win, bf16[2,4,56,256]{3,2,1,0:T(8,128)(2,1)} %get-tuple-element.36.edge, ...), custom_call_target="tpu_custom_call" | custom-call | tf_op jit(solution)/shard_map/merge/pallas_call | solution.py:477
  80.3 68.5 %backward.1 = (bf16[48,256,128]{2,1,0:T(8,128)(2,1)}, bf16[14,14,4,512]{3,2,1,0:T(4,128)(2,1)}, bf16[7,28,16,256]{3,2,1,0:T(8,128)(2,1)}) custom-call(bf16[8,392,256]{2,1,0:T(8,128)(2,1)} %get-tuple-element.38.grad_out, bf16[8,392,256]{2,1,0:T(8,128)(2,1)} %get-tuple-element.39.x_in, bf16[8,768,392]{2,1,0:T(8,128)(2,1)} %get-tuple-element.40.qkv_in, ...), custom_call_target="tpu_custom_call" | custom-call | tf_op jit(solution)/shard_map/backward/pallas_call | solution.py:667
  148.8 0.0 copy-start
  148.8 1.9 copy-done
  150.7 41.4 %sum_all.1 = bf16[12288,128]{1,0:T(8,128)(2,1)S(1)} custom-call(bf16[12288,128]{1,0:T(8,128)(2,1)S(1)} %bitcast.18), custom_call_target="tpu_custom_call" | custom-call | tf_op jit(solution)/shard_map/sum_all/pallas_call | solution.py:827
  192.1 0.0 copy-start.2
  192.2 0.0 copy-start.1
  192.2 2.7 %spread.1 = (f32[256,768]{1,0:T(8,128)}, f32[256,256]{1,0:T(8,128)}, f32[256,1024]{1,0:T(8,128)}, f32[1024,256]{1,0:T(8,128)}, f32[1024,512]{1,0:T(8,128)}, /*index=5*/f32[16,128]{1,0:T(8,128)S(1)}) custom-call(bf16[48,256,128]{2,1,0:T(8,128)(2,1)S(1)} %bitcast.17), custom_call_target="tpu_custom_call" | custom-call | tf_op jit(solution)/shard_map/spread/pallas_call | solution.py:856
  194.8 0.6 slice_bitcast_fusion.1
  195.4 0.6 slice_bitcast_fusion
  196.0 0.0 copy-done.2
  196.0 0.9 copy.23
  196.9 0.0 copy-done.1
  196.9 1.2 copy.24
  (3 shorter events, 0.0 us)
Async XLA Ops:
  148.8 1.9 copy-start
  192.1 3.8 %copy-start.2 = (bf16[14,14,4,512]{3,2,1,0:T(4,128)(2,1)S(1)}, bf16[14,14,4,512]{3,2,1,0:T(4,128)(2,1)}, u32[]{:S(2)}) copy-start(bf16[14,14,4,512]{3,2,1,0:T(4,128)(2,1)} %get-tuple-element.51) | copy-start | bytes 2408452
  192.2 4.7 %copy-start.1 = (bf16[7,28,16,256]{3,2,1,0:T(8,128)(2,1)S(1)}, bf16[7,28,16,256]{3,2,1,0:T(8,128)(2,1)}, u32[]{:S(2)}) copy-start(bf16[7,28,16,256]{3,2,1,0:T(8,128)(2,1)} %get-tuple-element.52) | copy-start | bytes 4816900

commit v2 on v1

--- a/solution.py
+++ b/solution.py
@@ -388,10 +388,13 @@
             blocks[first + a * (width // 128) + b] = part.astype(BF16)
 
 
-def from_blocks(blocks, first, height, width):
-    rows, cols = height // 256, width // 128
-    part = blocks[first : first + rows * cols].reshape(rows, cols, 256, 128)
-    return part.transpose(0, 2, 1, 3).reshape(height, width).astype(F32)
+def store_blocks(flat, first, values):
+    height, width = values.shape
+    for a in range(height // 256):
+        for b in range(width // 128):
+            at = 256 * (first + a * (width // 128) + b)
+            part = values[256 * a : 256 * (a + 1), 128 * b : 128 * (b + 1)]
+            flat[at : at + 256] = part.astype(BF16)
 
 
 def column_runs(wc):
@@ -497,16 +500,186 @@
     )(out_win, edge, gm, gain3, reduce_w, place)
 
 
+ORDERS = (("x", "y", "z"), ("y", "z", "x"), ("z", "x", "y"))
+
+
+def torus(n_tm):
+    return {32: (4, 2, 4), 4: (2, 1, 2)}[n_tm]
+
+
+class Torus:
+    def __init__(self, dims):
+        self.dims = dims
+        _, n_yl, n_z = dims
+        m, r = lax.axis_index("tm"), lax.axis_index("rows")
+        self.core = lax.rem(r, 2)
+        self.size = dims[0]
+        self.at = {
+            "x": m // (n_yl * n_z),
+            "y": (r // 2) * n_yl + lax.rem(m // n_z, n_yl),
+            "z": lax.rem(m, n_z),
+        }
+
+    def device(self, core=None, **moved):
+        _, n_yl, n_z = self.dims
+        at = {**self.at, **moved}
+        core = self.core if core is None else core
+        m = (at["x"] * n_yl + lax.rem(at["y"], n_yl)) * n_z + at["z"]
+        return (m, (at["y"] // n_yl) * 2 + core)
+
+    def partners(self, axis):
+        places = [lax.rem(self.at[axis] + j, self.size) for j in range(1, self.size)]
+        return [(place, self.device(**{axis: place})) for place in places]
+
+    def other(self):
+        return self.device(core=1 - self.core)
+
+    def everyone(self):
+        return [self.other()] + [dev for axis in "xyz" for _, dev in self.partners(axis)]
+
+
+def at_rows(start, length):
+    return pl.ds(pl.multiple_of(start, 16), length)
+
+
+class Sum:
+    def __init__(self, here, lengths, whole_last, source, total, base, scratch):
+        self.here, self.lengths, self.whole_last = here, lengths, whole_last
+        self.source, self.total, self.base = source, total, base
+        self.core_in, *rest = scratch
+        self.accs, self.ins = rest[0:3], rest[3:6]
+        self.core_sems, self.rs_sems, self.ag_sems, self.back_sems = (
+            tuple(rest[6 + 2 * n : 8 + 2 * n]) for n in range(4)
+        )
+
+    @staticmethod
+    def scratch(size, lengths, whole_last):
+        most, length = max(lengths), max(lengths)
+        shapes = [(3, most, 128)]
+        accs, ins = [], []
+        for s in range(3):
+            accs.append((3, length, 128))
+            length = length if s == 2 and whole_last else length // size
+            ins.append((3, size - 1, length, 128))
+        sems = [(3,), (3,), (9 * (size - 1),), (9 * (size - 1),), (9 * (size - 1),), (9 * (size - 1),), (3,), (3,)]
+        return [pltpu.VMEM(shape, BF16) for shape in shapes + accs + ins] + [DMA(n) for n in sems]
+
+    def half(self, core, p):
+        return core * sum(self.lengths) + sum(self.lengths[:p])
+
+    def piece(self, p, s):
+        start, length = self.half(self.here.core, p), self.lengths[p]
+        for n in range(s):
+            if not (n == 2 and self.whole_last):
+                length = length // self.here.size
+                start = start + self.here.at[ORDERS[p][n]] * length
+        return start, length
+
+    def core_copy(self, p):
+        start = self.half(1 - self.here.core, p)
+        return remote(
+            self.source.at[at_rows(start, self.lengths[p])],
+            self.core_in.at[p, 0 : self.lengths[p]],
+            self.core_sems, p, self.here.other(),
+        )
+
+    def rs_copies(self, p, s):
+        _, length = self.piece(p, s)
+        whole_piece = s == 3 and self.whole_last
+        return [
+            remote(
+                self.accs[s - 1].at[p, 0:length]
+                if whole_piece
+                else self.accs[s - 1].at[p, at_rows(place * length, length)],
+                self.ins[s - 1].at[p, j, 0:length],
+                self.rs_sems, (3 * (s - 1) + p) * (self.here.size - 1) + j, dev,
+            )
+            for j, (place, dev) in enumerate(self.here.partners(ORDERS[p][s - 1]))
+        ]
+
+    def ag_copies(self, p, s):
+        start, length = self.piece(p, s)
+        region = self.total.at[at_rows(self.base + start, length)]
+        return [
+            remote(region, region, self.ag_sems, (3 * (s - 1) + p) * (self.here.size - 1) + j, dev)
+            for j, (_, dev) in enumerate(self.here.partners(ORDERS[p][s - 1]))
+        ]
+
+    def back_copy(self, p):
+        start, length = self.piece(p, 0)
+        region = self.total.at[at_rows(self.base + start, length)]
+        return remote(region, region, self.back_sems, p, self.here.other())
+
+    def start(self):
+        for p in range(3):
+            self.core_copy(p).start()
+
+    def reduce(self, s):
+        for p in range(3):
+            start, length = self.piece(p, s)
+            if s == 0:
+                self.core_copy(p).wait_recv()
+                value = self.source[at_rows(start, length)].astype(F32)
+                value = value + self.core_in[p, 0:length].astype(F32)
+            else:
+                for copy in self.rs_copies(p, s):
+                    copy.wait_recv()
+                if s == 3 and self.whole_last:
+                    value = self.accs[2][p, 0:length].astype(F32)
+                else:
+                    place = self.here.at[ORDERS[p][s - 1]]
+                    value = self.accs[s - 1][p, at_rows(place * length, length)].astype(F32)
+                for j in range(self.here.size - 1):
+                    value = value + self.ins[s - 1][p, j, 0:length].astype(F32)
+            if s < 3:
+                self.accs[s][p, 0:length] = value.astype(BF16)
+                for copy in self.rs_copies(p, s + 1):
+                    copy.start()
+            else:
+                self.total[at_rows(self.base + start, length)] = value.astype(BF16)
+                for copy in self.ag_copies(p, 2 if self.whole_last else 3):
+                    copy.start()
+
+    def gather(self, s):
+        for p in range(3):
+            for copy in self.ag_copies(p, s):
+                copy.wait_recv()
+            for copy in self.ag_copies(p, s - 1) if s > 1 else [self.back_copy(p)]:
+                copy.start()
+
+    def finish(self):
+        for p in range(3):
+            self.back_copy(p).wait()
+            self.core_copy(p).wait_send()
+            for s in (1, 2, 3):
+                for copy in self.rs_copies(p, s):
+                    copy.wait_send()
+                if s < 3 or not self.whole_last:
+                    for copy in self.ag_copies(p, s):
+                        copy.wait_send()
+
+
+EARLY, LATE = (2048, 2048, 1024), (512, 256, 256)
+EARLY_ROWS, LATE_ROWS = 2 * sum(EARLY), 2 * sum(LATE)
+
+
 def backward_kernel(
-    grad_out, x_in, qkv_in, exp_in, inv_in, att_in, hid_in, act_in, slope_in,
+    dims, grad_out, att_a, hid_in, act_in, slope_in, x_in, qkv_in, exp_in, inv_in, att_in,
     qkv_t, proj, gain1, gain2, up_w, down_w, reduce_blocks, grad_gain3, pieces,
-    blocks, merged, grad_tokens,
-    grad_rows_t, grad_qkv_t, grad_proj, grad_up, grad_down_t, grad_gain1, grad_gain2,
-    late, final, pack_t, halo_t, t_out, t_in, row_out, row_in, own_sem, m_out, m_in, m_own,
+    totals, merged, grad_tokens,
+    grad_hidden_all, grad_att_all, grad_rows_t, grad_qkv_t, grad_proj, grad_up, grad_down_t,
+    grad_gain1, grad_gain2, late, final, pack_t, halo_t, early_blocks, late_blocks, total,
+    t_out, t_in, row_out, row_in, own_sem, m_out, m_in, m_own, total_sem, *sum_scratch,
 ):
-    tw, wc = 1 - pl.program_id(0), pl.program_id(1)
-    place = Place()
+    step = pl.program_id(0)
+    tw, wc = 1 - lax.rem(step, 8) // 4, lax.rem(step, 4)
+    window = 4 * tw + wc
+    first_phase, second_phase = step < 8, step >= 8
+    place, here = Place(), Torus(dims)
     t_sems, row_sems, m_sems = (t_out, t_in), (row_out, row_in), (m_out, m_in)
+    half = len(sum_scratch) // 2
+    early_sum = Sum(here, EARLY, False, early_blocks, total, 0, sum_scratch[:half])
+    late_sum = Sum(here, LATE, True, late_blocks, total, EARLY_ROWS, sum_scratch[half:])
 
     def m_ends(k, n):
         c = lax.rem(place.r + k + 3, 4)
@@ -544,23 +717,33 @@
 
     def row_copy(at):
         a, b, n = RUNS[at]
-        window, first = (at, 0) if at < 3 else (3, b - 21)
+        part, first = (at, 0) if at < 3 else (3, b - 21)
         return remote(
-            final.at[window, 4:7, first : first + n], grad_tokens.at[0:3, a : a + n],
+            final.at[part, 4:7, first : first + n], grad_tokens.at[0:3, a : a + n],
             row_sems, at, place.at(0, 1),
         )
 
     def own_copy(at):
         a, b, n = RUNS[at]
-        window, first = (at, 0) if at < 3 else (3, b - 21)
+        part, first = (at, 0) if at < 3 else (3, b - 21)
         return pltpu.make_async_copy(
-            final.at[window, 0:4, first : first + n], grad_tokens.at[3:7, a : a + n], own_sem.at[at]
+            final.at[part, 0:4, first : first + n], grad_tokens.at[3:7, a : a + n], own_sem.at[at]
         )
 
-    @pl.when((tw == 1) & (wc == 0))
-    def _():
-        sources = [place.at(0, -1), place.at(-1, 0)]
-        place.greet(sources + [place.owner(k)[1] for k in (1, 2, 3)], place.owner(0)[1])
+    def total_copy(n):
+        start, length = ((0, EARLY_ROWS), (EARLY_ROWS, LATE_ROWS))[n]
+        region = pl.ds(start, length)
+        return pltpu.make_async_copy(total.at[region], totals.at[region], total_sem.at[n])
+
+    @pl.when(step == 0)
+    def _():
+        for ref in (grad_qkv_t, grad_proj, grad_up, grad_down_t, grad_gain1, grad_gain2):
+            ref[...] = jnp.zeros_like(ref)
+        sources = [place.at(0, -1), place.at(-1, 0)] + [place.owner(k)[1] for k in (1, 2, 3)]
+        place.greet(sources + here.everyone(), place.owner(0)[1])
+
+    @pl.when(step == 1)
+    def _():
         m_each(lambda k, n: m_copy(k, n).start(), lambda n: m_local(n).start())
 
         @pl.when(place.odd == 1)
@@ -569,78 +752,111 @@
                 m_copy(k, 2).start()
             m_local(2).start()
 
-        for ref in (grad_qkv_t, grad_proj, grad_up, grad_down_t, grad_gain1, grad_gain2):
-            ref[...] = jnp.zeros_like(ref)
-
-    grad_rows = grad_out[0]
-    normed2, inverse2 = norm_forward(hid_in[0].astype(F32))
-    second_in = (normed2 * gain2[...]).astype(BF16)
-    grad_second = jnp.zeros((NPOS, C), F32)
+    @pl.when(first_phase)
+    def _():
+        grad_rows = grad_out[0]
+        normed2, inverse2 = norm_forward(hid_in[0].astype(F32))
+        second_in = (normed2 * gain2[...]).astype(BF16)
+        grad_second = jnp.zeros((NPOS, C), F32)
+        for part in range(4):
+            cols = slice(256 * part, 256 * (part + 1))
+            grad_down_t[:, cols] += dot_tn(grad_rows, act_in[0, :, cols])
+            grad_act = dot_nt(grad_rows, down_w[cols])
+            grad_up_in = (grad_act * slope_in[0, :, cols].astype(F32)).astype(BF16)
+            grad_up[:, cols] += dot_tn(second_in, grad_up_in)
+            grad_second = grad_second + dot_nt(grad_up_in, up_w[:, cols])
+        grad_gain2[...] += jnp.sum(grad_second * normed2, axis=0, keepdims=True)
+        back = norm_backward(normed2, inverse2, gain2[...], grad_second)
+        grad_hidden = grad_rows.astype(F32) + back
+        grad_hidden_all[window] = grad_hidden
+        grad_hidden_b = grad_hidden.astype(BF16)
+        grad_proj[...] += dot_nn(att_a[0], grad_hidden_b)
+        grad_att_all[window] = dot_nt(proj[...], grad_hidden_b).astype(BF16)
+
+    @pl.when(step == 7)
+    def _():
+        flat = early_blocks
+        store_blocks(flat, 16, grad_up[...])
+        store_blocks(flat, 24, grad_down_t[...].T)
+        store_blocks(flat, 32, grad_proj[...])
+        flat[0:4096] = reduce_blocks[...].reshape(4096, 128)
+        rows = [grad_gain2[:, 0:128], grad_gain2[:, 128:256]]
+        rows += [grad_gain3[:, 128 * n : 128 * (n + 1)] for n in range(8)]
+        rows.append(jnp.zeros((6, 128), F32))
+        flat[34 * 256 : 34 * 256 + 16] = jnp.concatenate(rows, axis=0).astype(BF16)
+        flat[34 * 256 + 16 :] = jnp.zeros((EARLY_ROWS - 34 * 256 - 16, 128), BF16)
+        early_sum.start()
+
+    for at, run in (
+        (9, lambda: early_sum.reduce(0)),
+        (11, lambda: early_sum.reduce(1)),
+        (12, lambda: early_sum.reduce(2)),
+        (13, lambda: early_sum.reduce(3)),
+        (14, lambda: early_sum.gather(3)),
+        (15, lambda: early_sum.gather(2)),
+    ):
+        pl.when(step == at)(run)
+
+    @pl.when(second_phase)
+    def _():
+        for h in range(HEADS):
+            at_q = slice(HEAD * h, HEAD * (h + 1))
+            at_k = slice(C + HEAD * h, C + HEAD * (h + 1))
+            at_v = slice(2 * C + HEAD * h, 2 * C + HEAD * (h + 1))
+            expon = exp_in[0, h]
+            incoming = grad_att_all[window, at_q].astype(F32) * inv_in[0, h : h + 1]
+            incoming = incoming.astype(BF16)
+            inner = incoming.astype(F32) * att_in[0, at_q].astype(F32)
+            inner = jnp.sum(inner, axis=0, keepdims=True)
+            grad_probs = dot_tn(qkv_in[0, at_v], incoming)
+            grad_scores = (expon.astype(F32) * (grad_probs - inner)).astype(BF16)
+            grad_rows_t[at_q] = (dot_nn(qkv_in[0, at_k], grad_scores) * SCALE).astype(BF16)
+            grad_rows_t[at_k] = (dot_nt(qkv_in[0, at_q], grad_scores) * LN2).astype(BF16)
+            grad_rows_t[at_v] = dot_nt(incoming, expon).astype(BF16)
+        normed1, inverse1 = norm_forward(x_in[0].astype(F32))
+        first_in = (normed1 * gain1[...]).astype(BF16)
+        grad_qkv_t[...] += dot_nn(grad_rows_t[...], first_in)
+        grad_first = dot_tn(grad_rows_t[...], qkv_t[...])
+        grad_gain1[...] += jnp.sum(grad_first * normed1, axis=0, keepdims=True)
+        back = norm_backward(normed1, inverse1, gain1[...], grad_first)
+        block = (grad_hidden_all[window] + back).reshape(49, 8, C)
+
+        @pl.when(tw == 1)
+        def _():
+            late[wc] = block[:, 0:4].astype(BF16)
+            pack_t[wc] = pack(block[:, 4:8])
+            t_copy(wc).start()
+
+        @pl.when(tw == 0)
+        def _():
+            t_copy(wc).wait_recv()
+            frames = jnp.concatenate([unpack(halo_t[wc]), block, late[wc].astype(F32)], axis=1)
+            final[wc] = frames.astype(BF16).reshape(7, 7, 16, C)
+
     for part in range(4):
-        cols = slice(256 * part, 256 * (part + 1))
-        grad_down_t[:, cols] += dot_tn(grad_rows, act_in[0, :, cols])
-        grad_act = dot_nt(grad_rows, down_w[cols])
-        grad_up_in = (grad_act * slope_in[0, :, cols].astype(F32)).astype(BF16)
-        grad_up[:, cols] += dot_tn(second_in, grad_up_in)
-        grad_second = grad_second + dot_nt(grad_up_in, up_w[:, cols])
-    grad_gain2[...] += jnp.sum(grad_second * normed2, axis=0, keepdims=True)
-    grad_hidden = grad_rows.astype(F32) + norm_backward(normed2, inverse2, gain2[...], grad_second)
-    grad_hidden_b = grad_hidden.astype(BF16)
-    grad_proj[...] += dot_nn(att_in[0], grad_hidden_b)
-    grad_att = dot_nt(proj[...], grad_hidden_b).astype(BF16)
-    for h in range(HEADS):
-        at_q = slice(HEAD * h, HEAD * (h + 1))
-        at_k = slice(C + HEAD * h, C + HEAD * (h + 1))
-        at_v = slice(2 * C + HEAD * h, 2 * C + HEAD * (h + 1))
-        expon = exp_in[0, h]
-        incoming = (grad_att[at_q].astype(F32) * inv_in[0, h : h + 1]).astype(BF16)
-        inner = jnp.sum(incoming.astype(F32) * att_in[0, at_q].astype(F32), axis=0, keepdims=True)
-        grad_probs = dot_tn(qkv_in[0, at_v], incoming)
-        grad_scores = (expon.astype(F32) * (grad_probs - inner)).astype(BF16)
-        grad_rows_t[at_q] = (dot_nn(qkv_in[0, at_k], grad_scores) * SCALE).astype(BF16)
-        grad_rows_t[at_k] = (dot_nt(qkv_in[0, at_q], grad_scores) * LN2).astype(BF16)
-        grad_rows_t[at_v] = dot_nt(incoming, expon).astype(BF16)
-    normed1, inverse1 = norm_forward(x_in[0].astype(F32))
-    first_in = (normed1 * gain1[...]).astype(BF16)
-    grad_qkv_t[...] += dot_nn(grad_rows_t[...], first_in)
-    grad_first = dot_tn(grad_rows_t[...], qkv_t[...])
-    grad_gain1[...] += jnp.sum(grad_first * normed1, axis=0, keepdims=True)
-    grad_x = grad_hidden + norm_backward(normed1, inverse1, gain1[...], grad_first)
-    block = grad_x.reshape(49, 8, C)
-
-    @pl.when(tw == 1)
-    def _():
-        late[wc] = block[:, 0:4].astype(BF16)
-        pack_t[wc] = pack(block[:, 4:8])
-        t_copy(wc).start()
-
-    @pl.when(tw == 0)
-    def _():
-        t_copy(wc).wait_recv()
-        frames = jnp.concatenate([unpack(halo_t[wc]), block, late[wc].astype(F32)], axis=1)
-        final[wc] = frames.astype(BF16).reshape(7, 7, 16, C)
-
-    for window in range(4):
-
-        @pl.when((tw == 0) & (wc == window))
-        def _(window=window):
-            for at in runs_of(window):
+
+        @pl.when(step == 12 + part)
+        def _(part=part):
+            for at in runs_of(part):
                 row_copy(at).start()
                 own_copy(at).start()
 
-    @pl.when((tw == 0) & (wc == 3))
-    def _():
-        blocks[0:16] = reduce_blocks[...]
-        to_blocks(blocks, 16, grad_up)
-        to_blocks(blocks, 24, grad_down_t[...].T)
-        to_blocks(blocks, 32, grad_qkv_t[...].T)
-        to_blocks(blocks, 38, grad_proj)
-        gains = [grad_gain1, grad_gain1, grad_gain2, grad_gain2] + [grad_gain3] * 8
-        lanes = [0, 1, 0, 1] + list(range(8))
-        rows = [ref[:, 128 * n : 128 * (n + 1)] for ref, n in zip(gains, lanes)]
-        blocks[40, 0:16] = jnp.concatenate(rows + [jnp.zeros((4, 128), F32)], axis=0).astype(BF16)
-        blocks[40, 16:256] = jnp.zeros((240, 128), BF16)
-        blocks[41:48] = jnp.zeros((7, 256, 128), BF16)
+    @pl.when(step == 15)
+    def _():
+        store_blocks(late_blocks, 0, grad_qkv_t[...].T)
+        rows = [grad_gain1[:, 0:128], grad_gain1[:, 128:256], jnp.zeros((14, 128), F32)]
+        late_blocks[1536:1552] = jnp.concatenate(rows, axis=0).astype(BF16)
+        late_blocks[1552:] = jnp.zeros((LATE_ROWS - 1552, 128), BF16)
+        late_sum.start()
+        late_sum.reduce(0)
+        early_sum.gather(1)
+        late_sum.reduce(1)
+        late_sum.reduce(2)
+        late_sum.reduce(3)
+        early_sum.finish()
+        total_copy(0).start()
+        late_sum.gather(2)
+        late_sum.gather(1)
         for at in range(5):
             row_copy(at).wait()
             own_copy(at).wait()
@@ -660,199 +876,86 @@
             for k in (1, 3):
                 m_copy(k, 2).wait_recv()
 
-
-def run_backward(grad_out, saved, *weights):
+        late_sum.finish()
+        total_copy(1).start()
+        total_copy(0).wait()
+        total_copy(1).wait()
+
+
+def run_backward(n_tm, grad_out, saved, *weights):
     sums = [(3 * C, C), (C, C), (C, HID), (C, HID), (1, C), (1, C)]
+    dims = torus(n_tm)
+    x, qkv, expon, inverse, att, hid, act, slope = saved
     *vmem_weights, _ = weights
+
+    def window(step):
+        return 4 * (1 - lax.rem(step, 8) // 4) + lax.rem(step, 4)
+
+    def in_first(array):
+        shape = array.shape[1:]
+        return pl.BlockSpec(
+            (1,) + shape, lambda s: (window(jnp.minimum(s, 7)),) + (0,) * len(shape)
+        )
+
+    def in_second(array):
+        shape = array.shape[1:]
+        return pl.BlockSpec(
+            (1,) + shape, lambda s: (window(jnp.maximum(s - 8, 0)),) + (0,) * len(shape)
+        )
+
+    first, second = (grad_out, att, hid, act, slope), (x, qkv, expon, inverse, att)
     return pl.pallas_call(
-        backward_kernel,
-        grid=(2, 4),
+        lambda *refs: backward_kernel(dims, *refs),
+        grid=(16,),
         out_shape=[
-            jax.ShapeDtypeStruct((48, 256, 128), BF16),
+            jax.ShapeDtypeStruct((EARLY_ROWS + LATE_ROWS, 128), BF16),
             jax.ShapeDtypeStruct((14, 14, 4, C3), BF16),
             jax.ShapeDtypeStruct((7, 28, 16, C), BF16),
         ],
-        in_specs=[by_window(array.shape[1:], True) for array in (grad_out, *saved)]
+        in_specs=[in_first(array) for array in first]
+        + [in_second(array) for array in second]
         + [whole(w.shape) for w in vmem_weights]
         + [ANY_SPEC],
-        out_specs=[whole((48, 256, 128)), ANY_SPEC, ANY_SPEC],
-        scratch_shapes=[pltpu.VMEM((3 * C, NPOS), BF16)]
+        out_specs=[ANY_SPEC] * 3,
+        scratch_shapes=[
+            pltpu.VMEM((8, NPOS, C), F32),
+            pltpu.VMEM((8, C, NPOS), BF16),
+            pltpu.VMEM((3 * C, NPOS), BF16),
+        ]
         + [pltpu.VMEM(shape, F32) for shape in sums]
         + [
             pltpu.VMEM((4, 49, 4, C), BF16),
             pltpu.VMEM((4, 7, 7, 16, C), BF16),
             pltpu.VMEM((4, 13, 16, C), BF16),
             pltpu.VMEM((4, 13, 16, C), BF16),
+            pltpu.VMEM((EARLY_ROWS, 128), BF16),
+            pltpu.VMEM((LATE_ROWS, 128), BF16),
+            pltpu.VMEM((EARLY_ROWS + LATE_ROWS, 128), BF16),
             DMA((4,)), DMA((4,)), DMA((5,)), DMA((5,)), DMA((5,)), DMA((12,)), DMA((12,)), DMA((3,)),
-        ],
+            DMA((2,)),
+        ]
+        + Sum.scratch(dims[0], EARLY, False)
+        + Sum.scratch(dims[0], LATE, True),
         compiler_params=pltpu.CompilerParams(
             vmem_limit_bytes=58 * MIB, collective_id=2, has_side_effects=True
         ),
         name="backward",
-    )(grad_out, *saved, *weights)
-
-
-ORDERS = (("x", "y", "z"), ("y", "z", "x"), ("z", "x", "y"))
-PART = 2048
-
-
-def torus(n_tm):
-    return {32: (4, 2, 4), 8: (2, 2, 2), 4: (1, 2, 2), 2: (1, 2, 1)}[n_tm]
-
-
-class Torus:
-    def __init__(self, dims):
-        self.dims = dims
-        _, n_yl, n_z = dims
-        m, r = lax.axis_index("tm"), lax.axis_index("rows")
-        self.core = lax.rem(r, 2)
-        self.sizes = {"x": dims[0], "y": 2 * n_yl, "z": n_z}
-        self.at = {
-            "x": m // (n_yl * n_z),
-            "y": (r // 2) * n_yl + lax.rem(m // n_z, n_yl),
-            "z": lax.rem(m, n_z),
-        }
-
-    def device(self, core=None, **moved):
-        _, n_yl, n_z = self.dims
-        at = {**self.at, **moved}
-        core = self.core if core is None else core
-        m = (at["x"] * n_yl + lax.rem(at["y"], n_yl)) * n_z + at["z"]
-        return (m, (at["y"] // n_yl) * 2 + core)
-
-    def partners(self, axis):
-        size = self.sizes[axis]
-        places = [lax.rem(self.at[axis] + j, size) for j in range(1, size)]
-        return [(place, self.device(**{axis: place})) for place in places]
-
-
-def sum_kernel(dims, blocks, total, core_in, acc0, acc1, acc2, in1, in2, in3, *sems):
-    core_send, core_recv, rs_send, rs_recv, ag_send, ag_recv, back_send, back_recv = sems
-    here = Torus(dims)
-    other = here.device(core=1 - here.core)
-    everyone = [other] + [dev for axis in "xyz" for _, dev in here.partners(axis)]
-    barrier = pltpu.get_barrier_semaphore()
-    for dev in everyone:
-        pl.semaphore_signal(barrier, inc=1, device_id=dev, device_id_type=pl.DeviceIdType.MESH)
-    pl.semaphore_wait(barrier, len(everyone))
-
-    def send(src, dst, out_sem, in_sem, dev):
-        copy = pltpu.make_async_remote_copy(
-            src_ref=src, dst_ref=dst, send_sem=out_sem, recv_sem=in_sem,
-            device_id=dev, device_id_type=pl.DeviceIdType.MESH,
-        )
-        copy.start()
-        return copy
-
-    def rows(start, length):
-        return pl.ds(pl.multiple_of(start, length), length)
-
-    mine = here.core * (3 * PART)
-    theirs = (1 - here.core) * (3 * PART)
-    copies = [
-        send(
-            blocks.at[rows(theirs + p * PART, PART)], core_in.at[p],
-            core_send.at[p], core_recv.at[p], other,
-        )
-        for p in range(3)
-    ]
-    finished = list(copies)
-    accs, ins = (acc0, acc1, acc2), (in1, in2, in3)
-    in_flight = [[copy] for copy in copies]
-    starts = [mine + p * PART for p in range(3)]
-    lengths = [PART] * 3
-    regions = [[] for _ in range(3)]
-    for s in range(4):
-        for p in range(3):
-            for copy in in_flight[p]:
-                copy.wait_recv()
-            if s == 0:
-                value = blocks[rows(starts[p], PART)].astype(F32) + core_in[p].astype(F32)
-            else:
-                axis = ORDERS[p][s - 1]
-                place, length = here.at[axis], lengths[p] // here.sizes[axis]
-                value = accs[s - 1][p, rows(place * length, length)].astype(F32)
-                for j in range(here.sizes[axis] - 1):
-                    value = value + ins[s - 1][p, j].astype(F32)
-                starts[p] = starts[p] + place * length
-                lengths[p] = length
-            regions[p].append((starts[p], lengths[p]))
-            if s == 3:
-                total[rows(starts[p], lengths[p])] = value.astype(BF16)
-                continue
-            accs[s][p] = value.astype(BF16)
-            axis = ORDERS[p][s]
-            length = lengths[p] // here.sizes[axis]
-            in_flight[p] = [
-                send(
-                    accs[s].at[p, rows(place * length, length)], ins[s].at[p, j],
-                    rs_send.at[s, p, j], rs_recv.at[s, p, j], dev,
-                )
-                for j, (place, dev) in enumerate(here.partners(axis))
-            ]
-            finished += in_flight[p]
-
-    in_flight = [[], [], []]
-    for s in (3, 2, 1, 0):
-        for p in range(3):
-            for copy in in_flight[p]:
-                copy.wait_recv()
-            region = total.at[rows(*regions[p][s])]
-            if s == 0:
-                in_flight[p] = [send(region, region, back_send.at[p], back_recv.at[p], other)]
-            else:
-                in_flight[p] = [
-                    send(region, region, ag_send.at[s - 1, p, j], ag_recv.at[s - 1, p, j], dev)
-                    for j, (_, dev) in enumerate(here.partners(ORDERS[p][s - 1]))
-                ]
-            finished += in_flight[p]
-    for p in range(3):
-        for copy in in_flight[p]:
-            copy.wait_recv()
-    for copy in finished:
-        copy.wait_send()
-
-
-def run_sum(blocks, n_tm):
-    dims = torus(n_tm)
-    sizes = (dims[0], 2 * dims[1], dims[2])
-    assert min(sizes) == max(sizes) or n_tm != 32
-    lengths, ins = [PART], []
-    if min(sizes) == max(sizes):
-        for size in sizes:
-            lengths.append(lengths[-1] // size)
-            ins.append((3, size - 1, lengths[-1], 128))
-    sem = pltpu.SemaphoreType.DMA
-    most = max(sizes) - 1
-    return pl.pallas_call(
-        lambda *refs: sum_kernel(dims, *refs),
-        out_shape=jax.ShapeDtypeStruct((6 * PART, 128), BF16),
-        in_specs=[pl.BlockSpec(memory_space=pltpu.VMEM)],
-        out_specs=pl.BlockSpec(memory_space=pltpu.VMEM),
-        scratch_shapes=[pltpu.VMEM((3, PART, 128), BF16)]
-        + [pltpu.VMEM((3, length, 128), BF16) for length in lengths[:3]]
-        + [pltpu.VMEM(shape, BF16) for shape in ins]
-        + [sem((3,)), sem((3,)), sem((3, 3, most)), sem((3, 3, most)), sem((3, 3, most)), sem((3, 3, most))]
-        + [sem((3,)), sem((3,))],
-        compiler_params=pltpu.CompilerParams(
-            collective_id=0, has_side_effects=True, vmem_limit_bytes=32 * MIB
-        ),
-        name="sum_all",
-    )(blocks.reshape(6 * PART, 128)).reshape(48, 256, 128)
+    )(*first, *second, *weights)
 
 
 def spread_kernel(blocks, qkv, proj, up, down, reduce_w, gains):
-    for ref, first in ((qkv, 32), (proj, 38), (up, 16), (down, 24), (reduce_w, 0)):
+    for ref, first in ((qkv, 40), (proj, 32), (up, 16), (down, 24), (reduce_w, 0)):
         height, width = ref.shape
         for a in range(height // 256):
             for b in range(width // 128):
                 part = blocks[first + a * (width // 128) + b].astype(F32)
                 ref[256 * a : 256 * (a + 1), 128 * b : 128 * (b + 1)] = part
-    gains[...] = blocks[40, 0:16].astype(F32)
+    gains[0:16] = blocks[34, 0:16].astype(F32)
+    gains[16:32] = blocks[46, 0:16].astype(F32)
 
 
 def run_spread(blocks):
-    shapes = [(C, 3 * C), (C, C), (C, HID), (HID, C), (4 * C, C3), (16, 128)]
+    shapes = [(C, 3 * C), (C, C), (C, HID), (HID, C), (4 * C, C3), (32, 128)]
     return pl.pallas_call(
         spread_kernel,
         out_shape=[jax.ShapeDtypeStruct(shape, F32) for shape in shapes],
@@ -875,19 +978,18 @@
     grad_out, pieces, grad_reduce, grad_gain3 = run_merge(
         out_win, edge, gm, gain3, reduce_weight, place
     )
-    blocks, merged, grad_tokens = run_backward(
-        grad_out, saved, qkv_t, proj_weight, gain1, gain2, up_weight, down_weight, grad_reduce,
-        grad_gain3, pieces,
+    totals, merged, grad_tokens = run_backward(
+        n_tm, grad_out, saved, qkv_t, proj_weight, gain1, gain2, up_weight, down_weight,
+        grad_reduce, grad_gain3, pieces,
     )
-    *grads, gains = run_spread(run_sum(blocks, n_tm))
-    gains = gains.reshape(-1)
+    *grads, gains = run_spread(totals.reshape(48, 256, 128))
     return (
         merged.transpose(2, 0, 1, 3),
         grad_tokens.transpose(2, 0, 1, 3),
         *grads,
-        gains[0:256],
-        gains[256:512],
-        gains[512:1536],
+        gains[16:18].reshape(-1),
+        gains[0:2].reshape(-1),
+        gains[2:10].reshape(-1),
     )
 
 

time: 198 us -> 187 us (0.944)
  Pallas kernels: 191 us -> 180 us
    pallas_call x2 -> x1, Pallas kernels: 110 us -> 98.6 us  [run_backward(): pl.pallas_call(lambda *refs: backward_kernel(dims, *refs), grid=(16,), ou...]
where the time goes in v2:
time: 187 us
  Pallas kernels  180 us (96%)
  local copies, waits for them, and re-layouts  5.17 us (3%)
    pallas_call x1, Pallas kernels, run_backward(): pl.pallas_call(lambda *refs: backward_kernel(dims, *refs), grid=(16,), ou...  98.6 us
    pallas_call x1, Pallas kernels, run_forward(): pl.pallas_call(forward_kernel, grid=(2, 4), out_shape=[jax.ShapeDtypeStru...  68.5 us
    pallas_call x1, Pallas kernels, run_merge(): pl.pallas_call(merge_kernel, grid=(2,), out_shape=[jax.ShapeDtypeStruct((...  10.3 us
    unnamed x8, local copies, waits for them, and re-layouts  3.93 us

profile of v2, /device:TPU:1, one launch (start us, length us, event | category | flops | bytes accessed | tf_op | source)
XLA Modules:
  0.0 186.7 jit_solution(14571926156977909646)
XLA Ops:
  0.7 0.1 pad.3.clone
  0.8 0.7 add_convert_fusion.pos
  1.4 68.5 %forward.1 = (bf16[8,392,256]{2,1,0:T(8,128)(2,1)}, bf16[8,768,392]{2,1,0:T(8,128)(2,1)}, bf16[8,8,392,392]{3,2,1,0:T(8,128)(2,1)}, f32[8,8,392]{2,1,0:T(8,128)}...) custom-call(bf16[7,28,16,256]{3,2,1,0:T(8,128)(2,1)} %bitcast.17, ...), custom_call_target="tpu_custom_call" | custom-call | tf_op jit(solution)/shard_map/forward/pallas_call | solution.py:354
  70.0 10.3 %merge.1 = (bf16[8,392,256]{2,1,0:T(8,128)(2,1)}, bf16[4,4,14,4,512]{4,3,2,1,0:T(4,128)(2,1)}, bf16[16,256,128]{2,1,0:T(8,128)(2,1)}, f32[1,1024]{1,0:T(1,128)}) custom-call(bf16[8,392,256]{2,1,0:T(8,128)(2,1)} %get-tuple-element.35.out_win, bf16[2,4,56,256]{3,2,1,0:T(8,128)(2,1)} %get-tuple-element.36.edge, ...), custom_call_target="tpu_custom_call" | custom-call | tf_op jit(solution)/shard_map/merge/pallas_call | solution.py:480
  80.3 98.6 %backward.1 = (bf16[12288,128]{1,0:T(8,128)(2,1)}, bf16[14,14,4,512]{3,2,1,0:T(4,128)(2,1)}, bf16[7,28,16,256]{3,2,1,0:T(8,128)(2,1)}) custom-call(bf16[8,392,256]{2,1,0:T(8,128)(2,1)} %get-tuple-element.38.refs_0_, bf16[8,256,392]{2,1,0:T(8,128)(2,1)} %get-tuple-element.39.refs_1_.refs_9_, bf16[8,392,256]{2,1,0:T(8,128)(2,1)} %get-tuple-element.40.refs_2_, ...), custom_call_target="tpu_custom_call" | custom-call | tf_op jit(solution)/shard_map/backward/pallas_call | solution.py:907
  179.0 0.0 copy-start
  179.0 1.9 %copy-done = bf16[12288,128]{1,0:T(8,128)(2,1)S(1)} copy-done((bf16[12288,128]{1,0:T(8,128)(2,1)S(1)}, bf16[12288,128]{1,0:T(8,128)(2,1)}, u32[]{:S(2)}) %copy-start) | copy-done | bytes 3145752
  180.8 0.0 copy-start.2
  180.8 0.0 copy-start.1
  180.8 2.6 %spread.1 = (f32[256,768]{1,0:T(8,128)}, f32[256,256]{1,0:T(8,128)}, f32[256,1024]{1,0:T(8,128)}, f32[1024,256]{1,0:T(8,128)}, f32[1024,512]{1,0:T(8,128)}, /*index=5*/f32[32,128]{1,0:T(8,128)S(1)}) custom-call(bf16[48,256,128]{2,1,0:T(8,128)(2,1)S(1)} %bitcast.16), custom_call_target="tpu_custom_call" | custom-call | tf_op jit(solution)/shard_map/spread/pallas_call | solution.py:959
  183.5 0.6 slice_bitcast_fusion.1
  184.1 0.6 slice_bitcast_fusion
  184.7 0.0 copy-done.2
  184.7 0.9 copy.23
  185.6 0.0 copy-done.1
  185.6 1.2 copy.24
  (3 shorter events, 0.0 us)
Async XLA Ops:
  179.0 1.9 %copy-start = (bf16[12288,128]{1,0:T(8,128)(2,1)S(1)}, bf16[12288,128]{1,0:T(8,128)(2,1)}, u32[]{:S(2)}) copy-start(bf16[12288,128]{1,0:T(8,128)(2,1)} %get-tuple-element.53) | copy-start | bytes 9437188
  180.8 3.8 %copy-start.2 = (bf16[14,14,4,512]{3,2,1,0:T(4,128)(2,1)S(1)}, bf16[14,14,4,512]{3,2,1,0:T(4,128)(2,1)}, u32[]{:S(2)}) copy-start(bf16[14,14,4,512]{3,2,1,0:T(4,128)(2,1)} %get-tuple-element.51) | copy-start | bytes 2408452
  180.8 4.7 %copy-start.1 = (bf16[7,28,16,256]{3,2,1,0:T(8,128)(2,1)S(1)}, bf16[7,28,16,256]{3,2,1,0:T(8,128)(2,1)}, u32[]{:S(2)}) copy-start(bf16[7,28,16,256]{3,2,1,0:T(8,128)(2,1)} %get-tuple-element.52) | copy-start | bytes 4816900

commit v3 on v2

--- a/solution.py
+++ b/solution.py
@@ -52,9 +52,7 @@
 
 def gelu_and_slope(up):
     size = jnp.abs(up)
-    base = 1.0 + (0.3275911 * 0.7071067811865476) * size
-    guess = pl.reciprocal(base, approx=True)
-    t = guess * (2.0 - base * guess)
+    t = pl.reciprocal(1.0 + (0.3275911 * 0.7071067811865476) * size, approx=True)
     bell = jnp.exp2((-0.5 * LOG2E) * (up * up))
     series = 0.5 * 1.061405429 * t - 0.5 * 1.453152027
     series = series * t + 0.5 * 1.421413741
@@ -127,267 +125,6 @@
     return jnp.concatenate(parts, axis=1).reshape(52, 4, C)[0:49]
 
 
-def mask_rows(ids, pos, tw, wc):
-    lane = lax.broadcasted_iota(jnp.int32, (1, 28), 1)
-    first = lane == 7 * wc
-    here = (lane >= 7 * wc) & (lane < 7 * wc + 7)
-    frames = ids[0, pl.ds(pl.multiple_of(8 * tw, 8), 8), :]
-    rows = ids[:, pl.ds(pl.multiple_of(8 * tw, 8), 8), :]
-
-    def count(bits, kept):
-        kept_bits = jnp.where(kept, bits.astype(F32), 0.0)
-        return jnp.sum(jnp.sum(kept_bits, axis=0, keepdims=True), axis=1, keepdims=True)
-
-    past = [
-        count((frames >> 2) & 1, first),
-        count(jnp.concatenate([(rows[i, 0:1] >> 1) & 1 for i in range(7)], axis=0), first),
-        count(frames[0:1] & 1, here),
-    ]
-    bits = [
-        jnp.where(pos[n : n + 1] >= extent - past[n], 1.0, 0.0)
-        for n, extent in enumerate((8.0, 7.0, 7.0))
-    ]
-    none = [jnp.zeros((10, NPOS), F32)]
-    keys = jnp.concatenate([v for b in bits for v in (b, 1.0 - b)] + none, axis=0)
-    queries = jnp.concatenate([v for b in bits for v in (1.0 - b, b)] + none, axis=0) * -FAR
-    return keys.astype(BF16), queries.astype(BF16)
-
-
-def forward_kernel(
-    tokens, gm, ids, pos, qkv_w, proj, gain1, gain2, up_w, down_w,
-    x_out, qkv_out, exp_out, inv_out, att_out, hid_out, act_out, slope_out, out_out, qkv_t,
-    gm_in, edge_in,
-    tok, x_now, pack_t, halo_t, edge_out, own_sem, row_out, row_in, t_out, t_in, gm_out_sem, gm_in_sem,
-    gm_own, edge_out_sem, edge_in_sem,
-):
-    tw, wc = pl.program_id(0), pl.program_id(1)
-    place = Place()
-    row_sems, t_sems = (row_out, row_in), (t_out, t_in)
-    gm_sems, edge_sems = (gm_out_sem, gm_in_sem), (edge_out_sem, edge_in_sem)
-
-    def own_copies():
-        return [
-            pltpu.make_async_copy(
-                tokens.at[3:7, a : a + n], tok.at[0:4, b : b + n], own_sem.at[at]
-            )
-            for at, (a, b, n) in enumerate(((3, 0, 25), (0, 25, 3)))
-        ]
-
-    def row_copy(at):
-        a, b, n = RUNS[at]
-        return remote(
-            tokens.at[0:3, a : a + n], tok.at[4:7, b : b + n], row_sems, at, place.at(0, -1)
-        )
-
-    def t_copy():
-        return remote(pack_t.at[wc], halo_t.at[wc], t_sems, wc, place.at(-1, 0))
-
-    def gm_copy(k, part):
-        dev, _ = place.holder(k)
-        band = lax.rem(place.r + k, 4)
-        first = lax.rem(4 * band + 1 - band // 2 + 2 * part, 14)
-        slot = lax.rem(place.r + 3, 4)
-        src, dst = gm.at[pl.ds(first, 2)], gm_in.at[slot, 2 * part : 2 * part + 2]
-        return remote(src, dst, gm_sems, 2 * k + part, dev)
-
-    def gm_local(part):
-        band = place.r
-        first = lax.rem(4 * band + 1 - band // 2 + 2 * part, 14)
-        slot = lax.rem(place.r + 3, 4)
-        return pltpu.make_async_copy(
-            gm.at[pl.ds(first, 2)], gm_in.at[slot, 2 * part : 2 * part + 2], gm_own.at[part]
-        )
-
-    def edge_copy(half):
-        return remote(edge_out.at[half], edge_in.at[half], edge_sems, half, place.across())
-
-    @pl.when((tw == 0) & (wc == 0))
-    def _():
-        for copy in own_copies():
-            copy.start()
-        sources = [place.at(0, 1), place.at(1, 0), place.across()]
-        place.greet(sources + [place.holder(k)[1] for k in (1, 2, 3)], place.holder(0)[1])
-        for at in range(5):
-            row_copy(at).start()
-        qkv_t[...] = qkv_w[...].astype(F32).T.astype(BF16)
-        for copy in own_copies():
-            copy.wait()
-
-    @pl.when((tw == 0) & (wc == 1))
-    def _():
-        for k in (1, 2, 3):
-            for part in range(2):
-                gm_copy(k, part).start()
-
-        @pl.when(place.r == 0)
-        def _():
-            for part in range(2):
-                gm_copy(0, part).start()
-
-        @pl.when(place.r != 0)
-        def _():
-            for part in range(2):
-                gm_local(part).start()
-
-    for window in range(4):
-
-        @pl.when((tw == 0) & (wc == window))
-        def _(window=window):
-            for at in runs_of(window):
-                row_copy(at).wait_recv()
-
-    @pl.when(tw == 0)
-    def _():
-        block = tok[:, pl.ds(7 * wc, 7)].astype(F32).reshape(49, 16, C)
-        pack_t[wc] = pack(block[:, 0:4])
-        t_copy().start()
-        x_now[...] = block[:, 4:12]
-
-    @pl.when(tw == 1)
-    def _():
-        t_copy().wait_recv()
-        block = tok[:, pl.ds(7 * wc, 7)].astype(F32).reshape(49, 16, C)
-        x_now[...] = jnp.concatenate([block[:, 12:16], unpack(halo_t[wc])], axis=1)
-
-    x = x_now[...].reshape(NPOS, C)
-    x_out[0] = x.astype(BF16)
-    mask_k, mask_q = mask_rows(ids, pos, tw, wc)
-    normed, _ = norm_forward(x)
-    first_in = (normed * gain1[...]).astype(BF16)
-    rows = dot_nt(qkv_t[...], first_in)
-    qkv_out[0, 0:C] = (rows[0:C] * (SCALE * LOG2E)).astype(BF16)
-    qkv_out[0, C:] = rows[C:].astype(BF16)
-    for h in range(HEADS):
-        here = slice(HEAD * h, HEAD * (h + 1))
-        q = jnp.concatenate([qkv_out[0, HEAD * h : HEAD * (h + 1)], mask_q], axis=0)
-        k = jnp.concatenate([qkv_out[0, C + HEAD * h : C + HEAD * (h + 1)], mask_k], axis=0)
-        v = qkv_out[0, 2 * C + HEAD * h : 2 * C + HEAD * (h + 1)]
-        scores = dot_tn(k, q)
-        top = jnp.max(scores, axis=0, keepdims=True)
-        expon = jnp.exp2(scores - top)
-        inverse = 1.0 / jnp.sum(expon, axis=0, keepdims=True)
-        expon = expon.astype(BF16)
-        exp_out[0, h] = expon
-        inv_out[0, h : h + 1] = inverse
-        att_out[0, here] = (dot_nn(v, expon) * inverse).astype(BF16)
-    hidden = (x + dot_tn(att_out[0], proj[...])).astype(BF16)
-    hid_out[0] = hidden
-    hidden = hidden.astype(F32)
-    normed, _ = norm_forward(hidden)
-    second_in = (normed * gain2[...]).astype(BF16)
-    result = hidden
-    for part in range(4):
-        cols = slice(256 * part, 256 * (part + 1))
-        act, slope = gelu_and_slope(dot_nn(second_in, up_w[:, cols]))
-        act = act.astype(BF16)
-        act_out[0, :, cols] = act
-        slope_out[0, :, cols] = slope.astype(BF16)
-        result = result + dot_nn(act, down_w[cols])
-    out_out[0] = result.astype(BF16)
-    edge = jnp.where(place.odd == 1, result[336:392], result[0:56])
-    edge_out[tw, wc] = edge.astype(BF16)
-
-    @pl.when((tw == 0) & (wc == 3))
-    def _():
-        edge_copy(0).start()
-
-    @pl.when((tw == 1) & (wc == 3))
-    def _():
-        edge_copy(1).start()
-        for at in range(5):
-            row_copy(at).wait_send()
-        for n in range(4):
-            remote(pack_t.at[n], halo_t.at[n], t_sems, n, place.at(-1, 0)).wait_send()
-        for k in (1, 2, 3):
-            for part in range(2):
-                gm_copy(k, part).wait()
-
-        @pl.when(place.r == 0)
-        def _():
-            for part in range(2):
-                gm_copy(0, part).wait()
-
-        @pl.when(place.r != 0)
-        def _():
-            for part in range(2):
-                gm_local(part).wait()
-
-        for half in range(2):
-            edge_copy(half).wait()
-
-
-def whole(shape):
-    return pl.BlockSpec(shape, lambda *_: (0,) * len(shape))
-
-
-def by_window(shape, backwards=False):
-    def index(tw, wc):
-        return (4 * (1 - tw if backwards else tw) + wc,) + (0,) * len(shape)
-
-    return pl.BlockSpec((1,) + shape, index)
-
-
-SMEM_SPEC = pl.BlockSpec(memory_space=pltpu.SMEM)
-ANY_SPEC = pl.BlockSpec(memory_space=pl.ANY)
-DMA = pltpu.SemaphoreType.DMA
-
-
-def positions():
-    at = jnp.arange(NPOS)
-    rows = [at % 8, at // 56, (at // 8) % 7]
-    return jnp.concatenate([jnp.stack(rows), jnp.zeros((5, NPOS), at.dtype)]).astype(F32)
-
-
-def run_forward(tokens, gm, ids, qkv_w, proj, gain1, gain2, up_w, down_w):
-    saved = [
-        ((NPOS, C), BF16),
-        ((3 * C, NPOS), BF16),
-        ((HEADS, NPOS, NPOS), BF16),
-        ((HEADS, NPOS), F32),
-        ((C, NPOS), BF16),
-        ((NPOS, C), BF16),
-        ((NPOS, HID), BF16),
-        ((NPOS, HID), BF16),
-        ((NPOS, C), BF16),
-    ]
-    pos = positions()
-    return pl.pallas_call(
-        forward_kernel,
-        grid=(2, 4),
-        out_shape=[jax.ShapeDtypeStruct((8,) + shape, kind) for shape, kind in saved]
-        + [
-            jax.ShapeDtypeStruct((3 * C, C), BF16),
-            jax.ShapeDtypeStruct((4, 4, 14, 4, C3), BF16),
-            jax.ShapeDtypeStruct((2, 4, 56, C), BF16),
-        ],
-        in_specs=[ANY_SPEC, ANY_SPEC, whole(ids.shape), whole(pos.shape)]
-        + [whole(w.shape) for w in (qkv_w, proj, gain1, gain2, up_w, down_w)],
-        out_specs=[by_window(shape) for shape, _ in saved]
-        + [whole((3 * C, C)), ANY_SPEC, ANY_SPEC],
-        scratch_shapes=[
-            pltpu.VMEM((7, 28, 16, C), BF16),
-            pltpu.VMEM((49, 8, C), F32),
-            pltpu.VMEM((4, 13, 16, C), BF16),
-            pltpu.VMEM((4, 13, 16, C), BF16),
-            pltpu.VMEM((2, 4, 56, C), BF16),
-            DMA((2,)), DMA((5,)), DMA((5,)), DMA((4,)), DMA((4,)), DMA((8,)), DMA((8,)),
-            DMA((2,)), DMA((2,)), DMA((2,)),
-        ],
-        compiler_params=pltpu.CompilerParams(
-            vmem_limit_bytes=58 * MIB, collective_id=1, has_side_effects=True
-        ),
-        name="forward",
-    )(tokens, gm, ids, pos, qkv_w, proj, gain1, gain2, up_w, down_w)
-
-
-def to_blocks(blocks, first, values):
-    height, width = values.shape
-    for a in range(height // 256):
-        for b in range(width // 128):
-            part = values[256 * a : 256 * (a + 1), 128 * b : 128 * (b + 1)]
-            blocks[first + a * (width // 128) + b] = part.astype(BF16)
-
-
 def store_blocks(flat, first, values):
     height, width = values.shape
     for a in range(height // 256):
@@ -403,23 +140,13 @@
     return [(24, 0, 4), (0, 4, 7)]
 
 
-def merge_kernel(
-    out_win, edge, gm, gain3, reduce_w, place,
-    grad_out, m_all, reduce_blocks, grad_gain,
-    rows, third_all, gm_rows, grad_reduce,
+def merge_half(
+    tw, odd, out_all, edge, gm, gain3, reduce_w, grad_out, m_all, grad_gain, rows, third_all, gm_rows,
+    grad_reduce,
 ):
-    tw = pl.program_id(0)
-    r = place[0]
-    odd = lax.rem(r, 2)
-
-    @pl.when(tw == 0)
-    def _():
-        grad_reduce[...] = jnp.zeros_like(grad_reduce)
-        grad_gain[...] = jnp.zeros_like(grad_gain)
-
     for wc in range(4):
-        block = out_win[wc].astype(F32).reshape(7, 7, 8, C)
-        strip = edge[0, wc].astype(F32).reshape(7, 8, C)
+        block = out_all[4 * tw + wc].astype(F32).reshape(7, 7, 8, C)
+        strip = edge[tw, wc].astype(F32).reshape(7, 8, C)
         for start, first, last in column_runs(wc):
             cols = slice(start, start + last - first)
             rows[pl.ds(1 - odd, 7), cols] = block[:, first:last]
@@ -434,11 +161,12 @@
         ).reshape(112, 4 * C)
         normed, inverse = norm_forward(joined)
         third = normed * gain
-        merged = dot_nn(third.astype(BF16), reduce_w[...])
-        merged = merged.reshape(14, 8, C3)
-        m_all[0, a] = merged[:, 0:4].astype(BF16)
-        m_all[1, a] = merged[:, 4:8].astype(BF16)
-        grads = jnp.concatenate([gm[0, a].astype(F32), gm[1, a].astype(F32)], axis=1)
+        merged = dot_nn(third.astype(BF16), reduce_w[...]).reshape(14, 8, C3)
+        m_all[2 * tw, a] = merged[:, 0:4].astype(BF16)
+        m_all[2 * tw + 1, a] = merged[:, 4:8].astype(BF16)
+        grads = jnp.concatenate(
+            [gm[2 * tw, a].astype(F32), gm[2 * tw + 1, a].astype(F32)], axis=1
+        )
         grads = grads.reshape(112, C3).astype(BF16)
         gz = dot_nt(grads, reduce_w[...])
         gz_sum = jnp.sum(gz * normed, axis=0, keepdims=True)
@@ -465,39 +193,287 @@
             for start, first, last in column_runs(wc)
         ]
         block = runs[0] if len(runs) == 1 else jnp.concatenate(runs, axis=1)
-        grad_out[wc] = block.reshape(NPOS, C).astype(BF16)
+        grad_out[4 * tw + wc] = block.reshape(NPOS, C).astype(BF16)
+
+
+def mask_rows(ids, pos, tw, wc):
+    lane = lax.broadcasted_iota(jnp.int32, (1, 28), 1)
+    first = lane == 7 * wc
+    here = (lane >= 7 * wc) & (lane < 7 * wc + 7)
+    frames = ids[0, pl.ds(pl.multiple_of(8 * tw, 8), 8), :]
+    rows = ids[:, pl.ds(pl.multiple_of(8 * tw, 8), 8), :]
+
+    def count(bits, kept):
+        kept_bits = jnp.where(kept, bits.astype(F32), 0.0)
+        return jnp.sum(jnp.sum(kept_bits, axis=0, keepdims=True), axis=1, keepdims=True)
+
+    past = [
+        count((frames >> 2) & 1, first),
+        count(jnp.concatenate([(rows[i, 0:1] >> 1) & 1 for i in range(7)], axis=0), first),
+        count(frames[0:1] & 1, here),
+    ]
+    bits = [
+        jnp.where(pos[n : n + 1] >= extent - past[n], 1.0, 0.0)
+        for n, extent in enumerate((8.0, 7.0, 7.0))
+    ]
+    none = [jnp.zeros((10, NPOS), F32)]
+    keys = jnp.concatenate([v for b in bits for v in (b, 1.0 - b)] + none, axis=0)
+    queries = jnp.concatenate([v for b in bits for v in (1.0 - b, b)] + none, axis=0) * -FAR
+    return keys.astype(BF16), queries.astype(BF16)
+
+
+def forward_kernel(
+    tokens, gm, ids, pos, qkv_w, proj, gain1, gain2, up_w, down_w, gain3, reduce_w,
+    x_out, qkv_out, exp_out, inv_out, att_out, hid_out, act_out, slope_out, qkv_t, grad_out, m_all,
+    reduce_rows, grad_gain3,
+    tok, x_now, pack_t, halo_t, edge_out, edge_in, gm_in, out_all, rows_all, third_all, gm_rows,
+    grad_reduce, own_sem, row_out, row_in, t_out, t_in, gm_out_sem, gm_in_sem, gm_own, edge_out_sem,
+    edge_in_sem,
+):
+    step = pl.program_id(0)
+    tw, wc = step // 4, lax.rem(step, 4)
+    place = Place()
+    row_sems, t_sems = (row_out, row_in), (t_out, t_in)
+    gm_sems, edge_sems = (gm_out_sem, gm_in_sem), (edge_out_sem, edge_in_sem)
+
+    def own_copies():
+        return [
+            pltpu.make_async_copy(
+                tokens.at[3:7, a : a + n], tok.at[0:4, b : b + n], own_sem.at[at]
+            )
+            for at, (a, b, n) in enumerate(((3, 0, 25), (0, 25, 3)))
+        ]
+
+    def row_copy(at):
+        a, b, n = RUNS[at]
+        return remote(
+            tokens.at[0:3, a : a + n], tok.at[4:7, b : b + n], row_sems, at, place.at(0, -1)
+        )
+
+    def t_copy():
+        return remote(pack_t.at[wc], halo_t.at[wc], t_sems, wc, place.at(-1, 0))
+
+    def gm_copy(k, part):
+        dev, _ = place.holder(k)
+        band = lax.rem(place.r + k, 4)
+        first = lax.rem(4 * band + 1 - band // 2 + 2 * part, 14)
+        slot = lax.rem(place.r + 3, 4)
+        src, dst = gm.at[pl.ds(first, 2)], gm_in.at[slot, 2 * part : 2 * part + 2]
+        return remote(src, dst, gm_sems, 2 * k + part, dev)
+
+    def gm_local(part):
+        band = place.r
+        first = lax.rem(4 * band + 1 - band // 2 + 2 * part, 14)
+        slot = lax.rem(place.r + 3, 4)
+        return pltpu.make_async_copy(
+            gm.at[pl.ds(first, 2)], gm_in.at[slot, 2 * part : 2 * part + 2], gm_own.at[part]
+        )
+
+    def edge_copy(half):
+        return remote(edge_out.at[half], edge_in.at[half], edge_sems, half, place.across())
+
+    @pl.when((tw == 0) & (wc == 0))
+    def _():
+        for copy in own_copies():
+            copy.start()
+        sources = [place.at(0, 1), place.at(1, 0), place.across()]
+        place.greet(sources + [place.holder(k)[1] for k in (1, 2, 3)], place.holder(0)[1])
+        for at in range(5):
+            row_copy(at).start()
+        qkv_t[...] = qkv_w[...].astype(F32).T.astype(BF16)
+        for copy in own_copies():
+            copy.wait()
+
+    @pl.when((tw == 0) & (wc == 1))
+    def _():
+        for k in (1, 2, 3):
+            for part in range(2):
+                gm_copy(k, part).start()
+
+        @pl.when(place.r == 0)
+        def _():
+            for part in range(2):
+                gm_copy(0, part).start()
+
+        @pl.when(place.r != 0)
+        def _():
+            for part in range(2):
+                gm_local(part).start()
+
+    for window in range(4):
+
+        @pl.when((tw == 0) & (wc == window))
+        def _(window=window):
+            for at in runs_of(window):
+                row_copy(at).wait_recv()
+
+    @pl.when(tw == 0)
+    def _():
+        block = tok[:, pl.ds(7 * wc, 7)].astype(F32).reshape(49, 16, C)
+        pack_t[wc] = pack(block[:, 0:4])
+        t_copy().start()
+        x_now[...] = block[:, 4:12]
 
     @pl.when(tw == 1)
     def _():
-        to_blocks(reduce_blocks, 0, grad_reduce)
-
-
-def run_merge(out_win, edge, gm, gain3, reduce_w, place):
-    def by_tw(shape):
-        return pl.BlockSpec(shape, lambda tw: (tw,) + (0,) * (len(shape) - 1))
-
-    pieces = (2, 4, 14, 4, C3)
+        t_copy().wait_recv()
+        block = tok[:, pl.ds(7 * wc, 7)].astype(F32).reshape(49, 16, C)
+        x_now[...] = jnp.concatenate([block[:, 12:16], unpack(halo_t[wc])], axis=1)
+
+    @pl.when(step < 8)
+    def _():
+        x = x_now[...].reshape(NPOS, C)
+        x_out[0] = x.astype(BF16)
+        mask_k, mask_q = mask_rows(ids, pos, tw, wc)
+        normed, _ = norm_forward(x)
+        first_in = (normed * gain1[...]).astype(BF16)
+        rows = dot_nt(qkv_t[...], first_in)
+        qkv_out[0, 0:C] = (rows[0:C] * (SCALE * LOG2E)).astype(BF16)
+        qkv_out[0, C:] = rows[C:].astype(BF16)
+        for h in range(HEADS):
+            here = slice(HEAD * h, HEAD * (h + 1))
+            q = jnp.concatenate([qkv_out[0, HEAD * h : HEAD * (h + 1)], mask_q], axis=0)
+            k = jnp.concatenate([qkv_out[0, C + HEAD * h : C + HEAD * (h + 1)], mask_k], axis=0)
+            v = qkv_out[0, 2 * C + HEAD * h : 2 * C + HEAD * (h + 1)]
+            scores = dot_tn(k, q)
+            top = jnp.max(scores, axis=0, keepdims=True)
+            expon = jnp.exp2(scores - top)
+            inverse = 1.0 / jnp.sum(expon, axis=0, keepdims=True)
+            expon = expon.astype(BF16)
+            exp_out[0, h] = expon
+            inv_out[0, h : h + 1] = inverse
+            att_out[0, here] = (dot_nn(v, expon) * inverse).astype(BF16)
+        hidden = (x + dot_tn(att_out[0], proj[...])).astype(BF16)
+        hid_out[0] = hidden
+        hidden = hidden.astype(F32)
+        normed, _ = norm_forward(hidden)
+        second_in = (normed * gain2[...]).astype(BF16)
+        result = hidden
+        for part in range(4):
+            cols = slice(256 * part, 256 * (part + 1))
+            act, slope = gelu_and_slope(dot_nn(second_in, up_w[:, cols]))
+            act = act.astype(BF16)
+            act_out[0, :, cols] = act
+            slope_out[0, :, cols] = slope.astype(BF16)
+            result = result + dot_nn(act, down_w[cols])
+        out_all[step] = result.astype(BF16)
+        edge = jnp.where(place.odd == 1, result[336:392], result[0:56])
+        edge_out[tw, wc] = edge.astype(BF16)
+
+    @pl.when((tw == 0) & (wc == 3))
+    def _():
+        edge_copy(0).start()
+
+    @pl.when(step == 7)
+    def _():
+        edge_copy(1).start()
+
+    @pl.when(step == 8)
+    def _():
+        grad_reduce[...] = jnp.zeros_like(grad_reduce)
+        grad_gain3[...] = jnp.zeros_like(grad_gain3)
+        for k in (1, 2, 3):
+            for part in range(2):
+                gm_copy(k, part).wait()
+
+        @pl.when(place.r == 0)
+        def _():
+            for part in range(2):
+                gm_copy(0, part).wait()
+
+        @pl.when(place.r != 0)
+        def _():
+            for part in range(2):
+                gm_local(part).wait()
+
+        edge_copy(0).wait()
+
+    @pl.when(step == 9)
+    def _():
+        edge_copy(1).wait()
+
+    @pl.when(step >= 8)
+    def _():
+        merge_half(
+            step - 8, place.odd, out_all, edge_in, gm_in, gain3, reduce_w, grad_out, m_all,
+            grad_gain3, rows_all, third_all, gm_rows, grad_reduce,
+        )
+
+    @pl.when(step == 9)
+    def _():
+        store_blocks(reduce_rows, 0, grad_reduce)
+        for at in range(5):
+            row_copy(at).wait_send()
+        for n in range(4):
+            remote(pack_t.at[n], halo_t.at[n], t_sems, n, place.at(-1, 0)).wait_send()
+
+
+def whole(shape):
+    return pl.BlockSpec(shape, lambda *_: (0,) * len(shape))
+
+
+def by_window(shape):
+    return pl.BlockSpec((1,) + shape, lambda s: (jnp.minimum(s, 7),) + (0,) * len(shape))
+
+
+ANY_SPEC = pl.BlockSpec(memory_space=pl.ANY)
+DMA = pltpu.SemaphoreType.DMA
+
+
+def positions():
+    at = jnp.arange(NPOS)
+    rows = [at % 8, at // 56, (at // 8) % 7]
+    return jnp.concatenate([jnp.stack(rows), jnp.zeros((5, NPOS), at.dtype)]).astype(F32)
+
+
+def run_forward(tokens, gm, ids, *weights):
+    saved = [
+        ((NPOS, C), BF16),
+        ((3 * C, NPOS), BF16),
+        ((HEADS, NPOS, NPOS), BF16),
+        ((HEADS, NPOS), F32),
+        ((C, NPOS), BF16),
+        ((NPOS, C), BF16),
+        ((NPOS, HID), BF16),
+        ((NPOS, HID), BF16),
+    ]
+    others = [
+        ((3 * C, C), BF16),
+        ((8, NPOS, C), BF16),
+        ((4, 4, 14, 4, C3), BF16),
+        ((4096, 128), BF16),
+        ((1, 4 * C), F32),
+    ]
+    pos = positions()
     return pl.pallas_call(
-        merge_kernel,
-        grid=(2,),
-        out_shape=[
-            jax.ShapeDtypeStruct((8, NPOS, C), BF16),
-            jax.ShapeDtypeStruct((4, 4, 14, 4, C3), BF16),
-            jax.ShapeDtypeStruct((16, 256, 128), BF16),
-            jax.ShapeDtypeStruct((1, 4 * C), F32),
-        ],
-        in_specs=[by_tw((4, NPOS, C)), by_tw((1, 4, 56, C)), by_tw(pieces)]
-        + [whole((1, 4 * C)), whole((4 * C, C3)), SMEM_SPEC],
-        out_specs=[by_tw((4, NPOS, C)), by_tw(pieces), whole((16, 256, 128)), whole((1, 4 * C))],
+        forward_kernel,
+        grid=(10,),
+        out_shape=[jax.ShapeDtypeStruct((8,) + shape, kind) for shape, kind in saved]
+        + [jax.ShapeDtypeStruct(shape, kind) for shape, kind in others],
+        in_specs=[ANY_SPEC, ANY_SPEC, whole(ids.shape), whole(pos.shape)]
+        + [whole(w.shape) for w in weights],
+        out_specs=[by_window(shape) for shape, _ in saved] + [whole(shape) for shape, _ in others],
         scratch_shapes=[
+            pltpu.VMEM((7, 28, 16, C), BF16),
+            pltpu.VMEM((49, 8, C), F32),
+            pltpu.VMEM((4, 13, 16, C), BF16),
+            pltpu.VMEM((4, 13, 16, C), BF16),
+            pltpu.VMEM((2, 4, 56, C), BF16),
+            pltpu.VMEM((2, 4, 56, C), BF16),
+            pltpu.VMEM((4, 4, 14, 4, C3), BF16),
+            pltpu.VMEM((8, NPOS, C), BF16),
             pltpu.VMEM((8, 28, 8, C), F32),
             pltpu.VMEM((448, 4 * C), BF16),
             pltpu.VMEM((448, C3), BF16),
             pltpu.VMEM((4 * C, C3), F32),
+            DMA((2,)), DMA((5,)), DMA((5,)), DMA((4,)), DMA((4,)), DMA((8,)), DMA((8,)),
+            DMA((2,)), DMA((2,)), DMA((2,)),
         ],
-        compiler_params=pltpu.CompilerParams(vmem_limit_bytes=58 * MIB),
-        name="merge",
-    )(out_win, edge, gm, gain3, reduce_w, place)
+        compiler_params=pltpu.CompilerParams(
+            vmem_limit_bytes=60 * MIB, collective_id=1, has_side_effects=True
+        ),
+        name="forward",
+    )(tokens, gm, ids, pos, *weights)
 
 
 ORDERS = (("x", "y", "z"), ("y", "z", "x"), ("z", "x", "y"))
@@ -659,16 +635,17 @@
                         copy.wait_send()
 
 
-EARLY, LATE = (2048, 2048, 1024), (512, 256, 256)
-EARLY_ROWS, LATE_ROWS = 2 * sum(EARLY), 2 * sum(LATE)
+SUMS = ((768, 768, 512), (1024, 768, 768), (512, 256, 256))
+SUM_ROWS = tuple(2 * sum(lengths) for lengths in SUMS)
+SUM_BASES = (0, SUM_ROWS[0], SUM_ROWS[0] + SUM_ROWS[1])
 
 
 def backward_kernel(
     dims, grad_out, att_a, hid_in, act_in, slope_in, x_in, qkv_in, exp_in, inv_in, att_in,
-    qkv_t, proj, gain1, gain2, up_w, down_w, reduce_blocks, grad_gain3, pieces,
+    qkv_t, proj, gain1, gain2, up_w, down_w, reduce_rows, grad_gain3, pieces,
     totals, merged, grad_tokens,
     grad_hidden_all, grad_att_all, grad_rows_t, grad_qkv_t, grad_proj, grad_up, grad_down_t,
-    grad_gain1, grad_gain2, late, final, pack_t, halo_t, early_blocks, late_blocks, total,
+    grad_gain1, grad_gain2, late, final, pack_t, halo_t, rows_0, rows_1, rows_2, total,
     t_out, t_in, row_out, row_in, own_sem, m_out, m_in, m_own, total_sem, *sum_scratch,
 ):
     step = pl.program_id(0)
@@ -677,9 +654,11 @@
     first_phase, second_phase = step < 8, step >= 8
     place, here = Place(), Torus(dims)
     t_sems, row_sems, m_sems = (t_out, t_in), (row_out, row_in), (m_out, m_in)
-    half = len(sum_scratch) // 2
-    early_sum = Sum(here, EARLY, False, early_blocks, total, 0, sum_scratch[:half])
-    late_sum = Sum(here, LATE, True, late_blocks, total, EARLY_ROWS, sum_scratch[half:])
+    each = len(sum_scratch) // 3
+    sum_0, sum_1, sum_2 = (
+        Sum(here, SUMS[n], True, rows, total, SUM_BASES[n], sum_scratch[each * n : each * (n + 1)])
+        for n, rows in enumerate((rows_0, rows_1, rows_2))
+    )
 
     def m_ends(k, n):
         c = lax.rem(place.r + k + 3, 4)
@@ -731,8 +710,7 @@
         )
 
     def total_copy(n):
-        start, length = ((0, EARLY_ROWS), (EARLY_ROWS, LATE_ROWS))[n]
-        region = pl.ds(start, length)
+        region = pl.ds(SUM_BASES[n], SUM_ROWS[n])
         return pltpu.make_async_copy(total.at[region], totals.at[region], total_sem.at[n])
 
     @pl.when(step == 0)
@@ -740,9 +718,11 @@
         for ref in (grad_qkv_t, grad_proj, grad_up, grad_down_t, grad_gain1, grad_gain2):
             ref[...] = jnp.zeros_like(ref)
         sources = [place.at(0, -1), place.at(-1, 0)] + [place.owner(k)[1] for k in (1, 2, 3)]
+        rows_0[...] = reduce_rows[...]
         place.greet(sources + here.everyone(), place.owner(0)[1])
-
-    @pl.when(step == 1)
+        sum_0.start()
+
+    @pl.when(step == 2)
     def _():
         m_each(lambda k, n: m_copy(k, n).start(), lambda n: m_local(n).start())
 
@@ -775,25 +755,29 @@
 
     @pl.when(step == 7)
     def _():
-        flat = early_blocks
-        store_blocks(flat, 16, grad_up[...])
-        store_blocks(flat, 24, grad_down_t[...].T)
-        store_blocks(flat, 32, grad_proj[...])
-        flat[0:4096] = reduce_blocks[...].reshape(4096, 128)
+        store_blocks(rows_1, 0, grad_up[...])
+        store_blocks(rows_1, 8, grad_down_t[...].T)
+        store_blocks(rows_1, 16, grad_proj[...])
         rows = [grad_gain2[:, 0:128], grad_gain2[:, 128:256]]
         rows += [grad_gain3[:, 128 * n : 128 * (n + 1)] for n in range(8)]
         rows.append(jnp.zeros((6, 128), F32))
-        flat[34 * 256 : 34 * 256 + 16] = jnp.concatenate(rows, axis=0).astype(BF16)
-        flat[34 * 256 + 16 :] = jnp.zeros((EARLY_ROWS - 34 * 256 - 16, 128), BF16)
-        early_sum.start()
+        rows_1[18 * 256 : 18 * 256 + 16] = jnp.concatenate(rows, axis=0).astype(BF16)
+        rows_1[18 * 256 + 16 :] = jnp.zeros((SUM_ROWS[1] - 18 * 256 - 16, 128), BF16)
+        sum_1.start()
 
     for at, run in (
-        (9, lambda: early_sum.reduce(0)),
-        (11, lambda: early_sum.reduce(1)),
-        (12, lambda: early_sum.reduce(2)),
-        (13, lambda: early_sum.reduce(3)),
-        (14, lambda: early_sum.gather(3)),
-        (15, lambda: early_sum.gather(2)),
+        (1, lambda: sum_0.reduce(0)),
+        (3, lambda: sum_0.reduce(1)),
+        (4, lambda: sum_0.reduce(2)),
+        (5, lambda: sum_0.reduce(3)),
+        (6, lambda: sum_0.gather(2)),
+        (8, lambda: sum_0.gather(1)),
+        (9, lambda: sum_1.reduce(0)),
+        (10, lambda: sum_1.reduce(1)),
+        (11, lambda: sum_1.reduce(2)),
+        (12, lambda: sum_1.reduce(3)),
+        (13, lambda: sum_1.gather(2)),
+        (14, lambda: sum_1.gather(1)),
     ):
         pl.when(step == at)(run)
 
@@ -843,20 +827,19 @@
 
     @pl.when(step == 15)
     def _():
-        store_blocks(late_blocks, 0, grad_qkv_t[...].T)
+        store_blocks(rows_2, 0, grad_qkv_t[...].T)
         rows = [grad_gain1[:, 0:128], grad_gain1[:, 128:256], jnp.zeros((14, 128), F32)]
-        late_blocks[1536:1552] = jnp.concatenate(rows, axis=0).astype(BF16)
-        late_blocks[1552:] = jnp.zeros((LATE_ROWS - 1552, 128), BF16)
-        late_sum.start()
-        late_sum.reduce(0)
-        early_sum.gather(1)
-        late_sum.reduce(1)
-        late_sum.reduce(2)
-        late_sum.reduce(3)
-        early_sum.finish()
+        rows_2[1536:1552] = jnp.concatenate(rows, axis=0).astype(BF16)
+        rows_2[1552:] = jnp.zeros((SUM_ROWS[2] - 1552, 128), BF16)
+        sum_2.start()
+        sum_0.finish()
+        sum_1.finish()
         total_copy(0).start()
-        late_sum.gather(2)
-        late_sum.gather(1)
+        total_copy(1).start()
+        for s in range(4):
+            sum_2.reduce(s)
+        sum_2.gather(2)
+        sum_2.gather(1)
         for at in range(5):
             row_copy(at).wait()
             own_copy(at).wait()
@@ -876,10 +859,10 @@
             for k in (1, 3):
                 m_copy(k, 2).wait_recv()
 
-        late_sum.finish()
-        total_copy(1).start()
-        total_copy(0).wait()
-        total_copy(1).wait()
+        sum_2.finish()
+        total_copy(2).start()
+        for n in range(3):
+            total_copy(n).wait()
 
 
 def run_backward(n_tm, grad_out, saved, *weights):
@@ -908,7 +891,7 @@
         lambda *refs: backward_kernel(dims, *refs),
         grid=(16,),
         out_shape=[
-            jax.ShapeDtypeStruct((EARLY_ROWS + LATE_ROWS, 128), BF16),
+            jax.ShapeDtypeStruct((sum(SUM_ROWS), 128), BF16),
             jax.ShapeDtypeStruct((14, 14, 4, C3), BF16),
             jax.ShapeDtypeStruct((7, 28, 16, C), BF16),
         ],
@@ -928,14 +911,11 @@
             pltpu.VMEM((4, 7, 7, 16, C), BF16),
             pltpu.VMEM((4, 13, 16, C), BF16),
             pltpu.VMEM((4, 13, 16, C), BF16),
-            pltpu.VMEM((EARLY_ROWS, 128), BF16),
-            pltpu.VMEM((LATE_ROWS, 128), BF16),
-            pltpu.VMEM((EARLY_ROWS + LATE_ROWS, 128), BF16),
+            *(pltpu.VMEM((n, 128), BF16) for n in (*SUM_ROWS, sum(SUM_ROWS))),
             DMA((4,)), DMA((4,)), DMA((5,)), DMA((5,)), DMA((5,)), DMA((12,)), DMA((12,)), DMA((3,)),
-            DMA((2,)),
+            DMA((3,)),
         ]
-        + Sum.scratch(dims[0], EARLY, False)
-        + Sum.scratch(dims[0], LATE, True),
+        + [shape for lengths in SUMS for shape in Sum.scratch(dims[0], lengths, True)],
         compiler_params=pltpu.CompilerParams(
             vmem_limit_bytes=58 * MIB, collective_id=2, has_side_effects=True
         ),
@@ -943,25 +923,55 @@
     )(*first, *second, *weights)
 
 
-def spread_kernel(blocks, qkv, proj, up, down, reduce_w, gains):
-    for ref, first in ((qkv, 40), (proj, 32), (up, 16), (down, 24), (reduce_w, 0)):
-        height, width = ref.shape
-        for a in range(height // 256):
-            for b in range(width // 128):
-                part = blocks[first + a * (width // 128) + b].astype(F32)
-                ref[256 * a : 256 * (a + 1), 128 * b : 128 * (b + 1)] = part
-    gains[0:16] = blocks[34, 0:16].astype(F32)
-    gains[16:32] = blocks[46, 0:16].astype(F32)
-
-
-def run_spread(blocks):
-    shapes = [(C, 3 * C), (C, C), (C, HID), (HID, C), (4 * C, C3), (32, 128)]
+def spread_kernel(
+    reduce_in, up_in, down_in, proj_in, qkv_in, gains_in, gain1_in,
+    qkv, proj, up, down, reduce_w, gain1, gain2, gain3,
+):
+    step = pl.program_id(0)
+    for ref, blocks in ((qkv, qkv_in), (up, up_in), (down, down_in), (reduce_w, reduce_in)):
+        for b in range(ref.shape[1] // 128):
+            ref[:, 128 * b : 128 * (b + 1)] = blocks[b].astype(F32)
+
+    @pl.when(step == 0)
+    def _():
+        for b in range(2):
+            proj[:, 128 * b : 128 * (b + 1)] = proj_in[b].astype(F32)
+        gains, first = gains_in[0, 0:16].astype(F32), gain1_in[0, 0:16].astype(F32)
+        for ref, rows, start in ((gain1, first, 0), (gain2, gains, 0), (gain3, gains, 2)):
+            for n in range(ref.shape[1] // 128):
+                ref[:, 128 * n : 128 * (n + 1)] = rows[start + n : start + n + 1]
+
+
+def run_spread(totals):
+    shapes = [(C, 3 * C), (C, C), (C, HID), (HID, C), (4 * C, C3), (1, C), (1, C), (1, 4 * C)]
+    wide = lambda count: pl.BlockSpec((256, 256), lambda s: (0, jnp.minimum(s, count - 1)))
+
+    def blocks(count, first, steps):
+        return pl.BlockSpec(
+            (count, 256, 128), lambda s: (first // count + jnp.minimum(s, steps - 1), 0, 0)
+        )
+
     return pl.pallas_call(
         spread_kernel,
+        grid=(4,),
         out_shape=[jax.ShapeDtypeStruct(shape, F32) for shape in shapes],
+        in_specs=[
+            blocks(4, 0, 4), blocks(2, 16, 4), blocks(2, 24, 4), blocks(2, 32, 1), blocks(2, 36, 3),
+            blocks(1, 34, 1), blocks(1, 42, 1),
+        ],
+        out_specs=[
+            wide(3),
+            whole((C, C)),
+            wide(4),
+            pl.BlockSpec((256, C), lambda s: (s, 0)),
+            pl.BlockSpec((256, C3), lambda s: (s, 0)),
+            whole((1, C)),
+            whole((1, C)),
+            whole((1, 4 * C)),
+        ],
         compiler_params=pltpu.CompilerParams(vmem_limit_bytes=32 * MIB),
         name="spread",
-    )(blocks)
+    )(*[totals] * 7)
 
 
 def local(
@@ -969,27 +979,24 @@
     gain_merge, reduce_weight, grad_merged,
 ):
     n_tm = lax.axis_size("tm")
-    place = lax.axis_index("rows").astype(jnp.int32).reshape(1)
     gain1, gain2, gain3 = (g.reshape(1, -1) for g in (gain_attn, gain_mlp, gain_merge))
-    *saved, out_win, qkv_t, gm, edge = run_forward(
+    *saved, qkv_t, grad_out, pieces, reduce_rows, grad_gain3 = run_forward(
         tokens.transpose(1, 2, 0, 3), grad_merged.transpose(1, 2, 0, 3),
         region_ids.transpose(1, 0, 2), qkv_weight, proj_weight, gain1, gain2, up_weight, down_weight,
-    )
-    grad_out, pieces, grad_reduce, grad_gain3 = run_merge(
-        out_win, edge, gm, gain3, reduce_weight, place
+        gain3, reduce_weight,
     )
     totals, merged, grad_tokens = run_backward(
         n_tm, grad_out, saved, qkv_t, proj_weight, gain1, gain2, up_weight, down_weight,
-        grad_reduce, grad_gain3, pieces,
+        reduce_rows, grad_gain3, pieces,
     )
-    *grads, gains = run_spread(totals.reshape(48, 256, 128))
+    *grads, gain1, gain2, gain3 = run_spread(totals.reshape(-1, 256, 128))
     return (
         merged.transpose(2, 0, 1, 3),
         grad_tokens.transpose(2, 0, 1, 3),
         *grads,
-        gains[16:18].reshape(-1),
-        gains[0:2].reshape(-1),
-        gains[2:10].reshape(-1),
+        gain1.reshape(-1),
+        gain2.reshape(-1),
+        gain3.reshape(-1),
     )
 
 

time: 187 us -> 193 us (1.032)
  Pallas kernels: 180 us -> 187 us
    pallas_call x1, Pallas kernels: 98.6 us -> 110 us  [run_backward(): pl.pallas_call(lambda *refs: backward_kernel(dims, *refs), grid=(16,), ou...]
    pallas_call x3 -> x2, Pallas kernels: 81.5 us -> 77 us  [the longest x1 74.2 us: run_forward(): pl.pallas_call(forward_kernel, grid=(10,), out_shape=[jax.ShapeDtypeStruc...]
where the time goes in v3:
time: 193 us
  Pallas kernels  187 us (97%)
  local copies, waits for them, and re-layouts  4.75 us (2%)
    pallas_call x1, Pallas kernels, run_backward(): pl.pallas_call(lambda *refs: backward_kernel(dims, *refs), grid=(16,), ou...  110 us
    pallas_call x1, Pallas kernels, run_forward(): pl.pallas_call(forward_kernel, grid=(10,), out_shape=[jax.ShapeDtypeStruc...  74.2 us
    unnamed x8, local copies, waits for them, and re-layouts  4.67 us

profile of v3, /device:TPU:1, one launch (start us, length us, event | category | flops | bytes accessed | tf_op | source)
XLA Modules:
  0.0 193.2 jit_solution(12542010966142113971)
XLA Ops:
  0.7 0.1 pad.3.clone
  0.8 0.7 add_convert_fusion.pos
  1.4 74.2 %forward.1 = (bf16[8,392,256]{2,1,0:T(8,128)(2,1)}, bf16[8,768,392]{2,1,0:T(8,128)(2,1)}, bf16[8,8,392,392]{3,2,1,0:T(8,128)(2,1)}, f32[8,8,392]{2,1,0:T(8,128)}...) custom-call(bf16[7,28,16,256]{3,2,1,0:T(8,128)(2,1)} %bitcast.19, ...), custom_call_target="tpu_custom_call" | custom-call | tf_op jit(solution)/shard_map/forward/pallas_call | solution.py:448
  75.6 110.0 %backward.1 = (bf16[11264,128]{1,0:T(8,128)(2,1)}, bf16[14,14,4,512]{3,2,1,0:T(4,128)(2,1)}, bf16[7,28,16,256]{3,2,1,0:T(8,128)(2,1)}) custom-call(bf16[8,392,256]{2,1,0:T(8,128)(2,1)} %get-tuple-element.34.refs_0_, bf16[8,256,392]{2,1,0:T(8,128)(2,1)} %get-tuple-element.35.refs_1_.refs_9_, bf16[8,392,256]{2,1,0:T(8,128)(2,1)} %get-tuple-element.36.refs_2_, ...), custom_call_target="tpu_custom_call" | custom-call | tf_op jit(solution)/shard_map/backward/pallas_call | solution.py:890
  185.6 0.0 copy-start
  185.6 1.8 copy-done
  187.4 0.0 copy-start.2
  187.4 2.9 %spread.1 = (f32[256,768]{1,0:T(8,128)}, f32[256,256]{1,0:T(8,128)}, f32[256,1024]{1,0:T(8,128)}, f32[1024,256]{1,0:T(8,128)}, f32[1024,512]{1,0:T(8,128)}, /*in...) custom-call(bf16[44,256,128]{2,1,0:T(8,128)(2,1)S(1)} %bitcast.12, bf16[44,256,128]{2,1,0:T(8,128)(2,1)S(1)} %bitcast.13, ...), custom_call_target="tpu_custom_call" | custom-call | tf_op jit(solution)/shard_map/spread/pallas_call | solution.py:954
  190.3 0.0 copy-start.1
  190.3 0.0 copy-done.2
  190.3 0.9 copy.23
  191.2 0.8 copy-done.1
  192.0 1.2 copy.24
  (3 shorter events, 0.0 us)
Async XLA Ops:
  185.6 1.8 copy-start
  187.4 2.9 %copy-start.2 = (bf16[14,14,4,512]{3,2,1,0:T(4,128)(2,1)S(1)}, bf16[14,14,4,512]{3,2,1,0:T(4,128)(2,1)}, u32[]{:S(2)}) copy-start(bf16[14,14,4,512]{3,2,1,0:T(4,128)(2,1)} %get-tuple-element.47) | copy-start | bytes 2408452
  190.3 1.7 copy-start.1

commit v4 on v3

--- a/solution.py
+++ b/solution.py
@@ -635,17 +635,18 @@
                         copy.wait_send()
 
 
-SUMS = ((768, 768, 512), (1024, 768, 768), (512, 256, 256))
+SUMS = ((2048, 2048, 1024), (512, 256, 256))
 SUM_ROWS = tuple(2 * sum(lengths) for lengths in SUMS)
-SUM_BASES = (0, SUM_ROWS[0], SUM_ROWS[0] + SUM_ROWS[1])
+SUM_BASES = (0, SUM_ROWS[0])
 
 
 def backward_kernel(
-    dims, grad_out, att_a, hid_in, act_in, slope_in, x_in, qkv_in, exp_in, inv_in, att_in,
+    dims, grad_out, att_a, hid_in, act_in, slope_in, x_in, qkv_in, inv_in, att_in, exp_hbm,
     qkv_t, proj, gain1, gain2, up_w, down_w, reduce_rows, grad_gain3, pieces,
     totals, merged, grad_tokens,
-    grad_hidden_all, grad_att_all, grad_rows_t, grad_qkv_t, grad_proj, grad_up, grad_down_t,
-    grad_gain1, grad_gain2, late, final, pack_t, halo_t, rows_0, rows_1, rows_2, total,
+    exp_two, grad_hidden_all, grad_att_all, grad_rows_t, grad_qkv_t, grad_proj, grad_up,
+    grad_down_t, grad_gain1, grad_gain2, late, final, pack_t, halo_t, early_rows, late_rows, total,
+    in_sem, exp_sem,
     t_out, t_in, row_out, row_in, own_sem, m_out, m_in, m_own, total_sem, *sum_scratch,
 ):
     step = pl.program_id(0)
@@ -654,11 +655,19 @@
     first_phase, second_phase = step < 8, step >= 8
     place, here = Place(), Torus(dims)
     t_sems, row_sems, m_sems = (t_out, t_in), (row_out, row_in), (m_out, m_in)
-    each = len(sum_scratch) // 3
-    sum_0, sum_1, sum_2 = (
+    each = len(sum_scratch) // 2
+    early, last = (
         Sum(here, SUMS[n], True, rows, total, SUM_BASES[n], sum_scratch[each * n : each * (n + 1)])
-        for n, rows in enumerate((rows_0, rows_1, rows_2))
+        for n, rows in enumerate((early_rows, late_rows))
     )
+
+    def reduce_copy():
+        return pltpu.make_async_copy(reduce_rows, early_rows.at[0:4096], in_sem.at[0])
+
+    def exp_copy(at):
+        source = 4 * (1 - lax.rem(at, 8) // 4) + lax.rem(at, 4)
+        slot = lax.rem(at, 2)
+        return pltpu.make_async_copy(exp_hbm.at[source], exp_two.at[slot], exp_sem.at[slot])
 
     def m_ends(k, n):
         c = lax.rem(place.r + k + 3, 4)
@@ -715,15 +724,11 @@
 
     @pl.when(step == 0)
     def _():
+        reduce_copy().start()
         for ref in (grad_qkv_t, grad_proj, grad_up, grad_down_t, grad_gain1, grad_gain2):
             ref[...] = jnp.zeros_like(ref)
         sources = [place.at(0, -1), place.at(-1, 0)] + [place.owner(k)[1] for k in (1, 2, 3)]
-        rows_0[...] = reduce_rows[...]
         place.greet(sources + here.everyone(), place.owner(0)[1])
-        sum_0.start()
-
-    @pl.when(step == 2)
-    def _():
         m_each(lambda k, n: m_copy(k, n).start(), lambda n: m_local(n).start())
 
         @pl.when(place.odd == 1)
@@ -755,39 +760,39 @@
 
     @pl.when(step == 7)
     def _():
-        store_blocks(rows_1, 0, grad_up[...])
-        store_blocks(rows_1, 8, grad_down_t[...].T)
-        store_blocks(rows_1, 16, grad_proj[...])
+        store_blocks(early_rows, 16, grad_up[...])
+        store_blocks(early_rows, 24, grad_down_t[...].T)
+        store_blocks(early_rows, 32, grad_proj[...])
         rows = [grad_gain2[:, 0:128], grad_gain2[:, 128:256]]
         rows += [grad_gain3[:, 128 * n : 128 * (n + 1)] for n in range(8)]
         rows.append(jnp.zeros((6, 128), F32))
-        rows_1[18 * 256 : 18 * 256 + 16] = jnp.concatenate(rows, axis=0).astype(BF16)
-        rows_1[18 * 256 + 16 :] = jnp.zeros((SUM_ROWS[1] - 18 * 256 - 16, 128), BF16)
-        sum_1.start()
+        early_rows[34 * 256 : 34 * 256 + 16] = jnp.concatenate(rows, axis=0).astype(BF16)
+        early_rows[34 * 256 + 16 :] = jnp.zeros((SUM_ROWS[0] - 34 * 256 - 16, 128), BF16)
+        reduce_copy().wait()
+        early.start()
 
     for at, run in (
-        (1, lambda: sum_0.reduce(0)),
-        (3, lambda: sum_0.reduce(1)),
-        (4, lambda: sum_0.reduce(2)),
-        (5, lambda: sum_0.reduce(3)),
-        (6, lambda: sum_0.gather(2)),
-        (8, lambda: sum_0.gather(1)),
-        (9, lambda: sum_1.reduce(0)),
-        (10, lambda: sum_1.reduce(1)),
-        (11, lambda: sum_1.reduce(2)),
-        (12, lambda: sum_1.reduce(3)),
-        (13, lambda: sum_1.gather(2)),
-        (14, lambda: sum_1.gather(1)),
+        (9, lambda: early.reduce(0)),
+        (11, lambda: early.reduce(1)),
+        (12, lambda: early.reduce(2)),
+        (13, lambda: early.reduce(3)),
+        (14, lambda: early.gather(2)),
     ):
         pl.when(step == at)(run)
 
+    @pl.when((step >= 7) & (step < 15))
+    def _():
+        exp_copy(step + 1).start()
+
     @pl.when(second_phase)
     def _():
+        exp_copy(step).wait()
+        slot = lax.rem(step, 2)
         for h in range(HEADS):
             at_q = slice(HEAD * h, HEAD * (h + 1))
             at_k = slice(C + HEAD * h, C + HEAD * (h + 1))
             at_v = slice(2 * C + HEAD * h, 2 * C + HEAD * (h + 1))
-            expon = exp_in[0, h]
+            expon = exp_two[slot, h]
             incoming = grad_att_all[window, at_q].astype(F32) * inv_in[0, h : h + 1]
             incoming = incoming.astype(BF16)
             inner = incoming.astype(F32) * att_in[0, at_q].astype(F32)
@@ -817,6 +822,14 @@
             frames = jnp.concatenate([unpack(halo_t[wc]), block, late[wc].astype(F32)], axis=1)
             final[wc] = frames.astype(BF16).reshape(7, 7, 16, C)
 
+    @pl.when(step == 15)
+    def _():
+        store_blocks(late_rows, 0, grad_qkv_t[...].T)
+        rows = [grad_gain1[:, 0:128], grad_gain1[:, 128:256], jnp.zeros((14, 128), F32)]
+        late_rows[1536:1552] = jnp.concatenate(rows, axis=0).astype(BF16)
+        late_rows[1552:] = jnp.zeros((SUM_ROWS[1] - 1552, 128), BF16)
+        last.start()
+
     for part in range(4):
 
         @pl.when(step == 12 + part)
@@ -827,19 +840,15 @@
 
     @pl.when(step == 15)
     def _():
-        store_blocks(rows_2, 0, grad_qkv_t[...].T)
-        rows = [grad_gain1[:, 0:128], grad_gain1[:, 128:256], jnp.zeros((14, 128), F32)]
-        rows_2[1536:1552] = jnp.concatenate(rows, axis=0).astype(BF16)
-        rows_2[1552:] = jnp.zeros((SUM_ROWS[2] - 1552, 128), BF16)
-        sum_2.start()
-        sum_0.finish()
-        sum_1.finish()
+        last.reduce(0)
+        early.gather(1)
+        last.reduce(1)
+        last.reduce(2)
+        last.reduce(3)
+        early.finish()
         total_copy(0).start()
-        total_copy(1).start()
-        for s in range(4):
-            sum_2.reduce(s)
-        sum_2.gather(2)
-        sum_2.gather(1)
+        last.gather(2)
+        last.gather(1)
         for at in range(5):
             row_copy(at).wait()
             own_copy(at).wait()
@@ -859,9 +868,9 @@
             for k in (1, 3):
                 m_copy(k, 2).wait_recv()
 
-        sum_2.finish()
-        total_copy(2).start()
-        for n in range(3):
+        last.finish()
+        total_copy(1).start()
+        for n in range(2):
             total_copy(n).wait()
 
 
@@ -869,7 +878,7 @@
     sums = [(3 * C, C), (C, C), (C, HID), (C, HID), (1, C), (1, C)]
     dims = torus(n_tm)
     x, qkv, expon, inverse, att, hid, act, slope = saved
-    *vmem_weights, _ = weights
+    *vmem_weights, _, grad_gain3, _ = weights
 
     def window(step):
         return 4 * (1 - lax.rem(step, 8) // 4) + lax.rem(step, 4)
@@ -883,10 +892,10 @@
     def in_second(array):
         shape = array.shape[1:]
         return pl.BlockSpec(
-            (1,) + shape, lambda s: (window(jnp.maximum(s - 8, 0)),) + (0,) * len(shape)
-        )
-
-    first, second = (grad_out, att, hid, act, slope), (x, qkv, expon, inverse, att)
+            (1,) + shape, lambda s: (window(jnp.maximum(s, 8)),) + (0,) * len(shape)
+        )
+
+    first, second = (grad_out, att, hid, act, slope), (x, qkv, inverse, att)
     return pl.pallas_call(
         lambda *refs: backward_kernel(dims, *refs),
         grid=(16,),
@@ -897,10 +906,12 @@
         ],
         in_specs=[in_first(array) for array in first]
         + [in_second(array) for array in second]
+        + [ANY_SPEC]
         + [whole(w.shape) for w in vmem_weights]
-        + [ANY_SPEC],
+        + [ANY_SPEC, whole(grad_gain3.shape), ANY_SPEC],
         out_specs=[ANY_SPEC] * 3,
         scratch_shapes=[
+            pltpu.VMEM((2, HEADS, NPOS, NPOS), BF16),
             pltpu.VMEM((8, NPOS, C), F32),
             pltpu.VMEM((8, C, NPOS), BF16),
             pltpu.VMEM((3 * C, NPOS), BF16),
@@ -912,15 +923,16 @@
             pltpu.VMEM((4, 13, 16, C), BF16),
             pltpu.VMEM((4, 13, 16, C), BF16),
             *(pltpu.VMEM((n, 128), BF16) for n in (*SUM_ROWS, sum(SUM_ROWS))),
+            DMA((1,)), DMA((2,)),
             DMA((4,)), DMA((4,)), DMA((5,)), DMA((5,)), DMA((5,)), DMA((12,)), DMA((12,)), DMA((3,)),
-            DMA((3,)),
+            DMA((2,)),
         ]
         + [shape for lengths in SUMS for shape in Sum.scratch(dims[0], lengths, True)],
         compiler_params=pltpu.CompilerParams(
             vmem_limit_bytes=58 * MIB, collective_id=2, has_side_effects=True
         ),
         name="backward",
-    )(*first, *second, *weights)
+    )(*first, *second, expon, *weights)
 
 
 def spread_kernel(
@@ -956,8 +968,8 @@
         grid=(4,),
         out_shape=[jax.ShapeDtypeStruct(shape, F32) for shape in shapes],
         in_specs=[
-            blocks(4, 0, 4), blocks(2, 16, 4), blocks(2, 24, 4), blocks(2, 32, 1), blocks(2, 36, 3),
-            blocks(1, 34, 1), blocks(1, 42, 1),
+            blocks(4, 0, 4), blocks(2, 16, 4), blocks(2, 24, 4), blocks(2, 32, 1), blocks(2, 40, 3),
+            blocks(1, 34, 1), blocks(1, 46, 1),
         ],
         out_specs=[
             wide(3),

time: 193 us -> 179 us (0.927)
  Pallas kernels: 187 us -> 172 us
    pallas_call x1, Pallas kernels: 110 us -> 95.3 us  [run_backward(): pl.pallas_call(lambda *refs: backward_kernel(dims, *refs), grid=(16,), ou...]
where the time goes in v4:
time: 179 us
  Pallas kernels  172 us (96%)
  local copies, waits for them, and re-layouts  4.82 us (3%)
    pallas_call x1, Pallas kernels, run_backward(): pl.pallas_call(lambda *refs: backward_kernel(dims, *refs), grid=(16,), ou...  95.3 us
    pallas_call x1, Pallas kernels, run_forward(): pl.pallas_call(forward_kernel, grid=(10,), out_shape=[jax.ShapeDtypeStruc...  74.2 us
    unnamed x8, local copies, waits for them, and re-layouts  4.74 us

profile of v4, /device:TPU:1, one launch (start us, length us, event | category | flops | bytes accessed | tf_op | source)
XLA Modules:
  0.0 178.5 jit_solution(11022099054482213510)
XLA Ops:
  0.7 0.1 pad.3.clone
  0.8 0.7 add_convert_fusion.pos
  1.4 74.2 %forward.1 = (bf16[8,392,256]{2,1,0:T(8,128)(2,1)}, bf16[8,768,392]{2,1,0:T(8,128)(2,1)}, bf16[8,8,392,392]{3,2,1,0:T(8,128)(2,1)}, f32[8,8,392]{2,1,0:T(8,128)}...) custom-call(bf16[7,28,16,256]{3,2,1,0:T(8,128)(2,1)} %bitcast.19, ...), custom_call_target="tpu_custom_call" | custom-call | tf_op jit(solution)/shard_map/forward/pallas_call | solution.py:448
  75.6 95.3 %backward.1 = (bf16[12288,128]{1,0:T(8,128)(2,1)}, bf16[14,14,4,512]{3,2,1,0:T(4,128)(2,1)}, bf16[7,28,16,256]{3,2,1,0:T(8,128)(2,1)}) custom-call(bf16[8,392,256]{2,1,0:T(8,128)(2,1)} %get-tuple-element.34.refs_0_, bf16[8,256,392]{2,1,0:T(8,128)(2,1)} %get-tuple-element.35.refs_1_.refs_8_, bf16[8,392,256]{2,1,0:T(8,128)(2,1)} %get-tuple-element.36.refs_2_, ...), custom_call_target="tpu_custom_call" | custom-call | tf_op jit(solution)/shard_map/backward/pallas_call | solution.py:899
  170.9 0.0 copy-start
  170.9 1.9 %copy-done = bf16[12288,128]{1,0:T(8,128)(2,1)S(1)} copy-done((bf16[12288,128]{1,0:T(8,128)(2,1)S(1)}, bf16[12288,128]{1,0:T(8,128)(2,1)}, u32[]{:S(2)}) %copy-start) | copy-done | bytes 3145752
  172.8 0.0 copy-start.2
  172.8 2.9 %spread.1 = (f32[256,768]{1,0:T(8,128)}, f32[256,256]{1,0:T(8,128)}, f32[256,1024]{1,0:T(8,128)}, f32[1024,256]{1,0:T(8,128)}, f32[1024,512]{1,0:T(8,128)}, /*in...) custom-call(bf16[48,256,128]{2,1,0:T(8,128)(2,1)S(1)} %bitcast.12, bf16[48,256,128]{2,1,0:T(8,128)(2,1)S(1)} %bitcast.13, ...), custom_call_target="tpu_custom_call" | custom-call | tf_op jit(solution)/shard_map/spread/pallas_call | solution.py:966
  175.7 0.0 copy-start.1
  175.7 0.0 copy-done.2
  175.7 0.9 copy.23
  176.5 0.8 copy-done.1
  177.4 1.2 copy.24
  (3 shorter events, 0.0 us)
Async XLA Ops:
  170.9 1.9 %copy-start = (bf16[12288,128]{1,0:T(8,128)(2,1)S(1)}, bf16[12288,128]{1,0:T(8,128)(2,1)}, u32[]{:S(2)}) copy-start(bf16[12288,128]{1,0:T(8,128)(2,1)} %get-tuple-element.49) | copy-start | bytes 9437188
  172.8 2.9 %copy-start.2 = (bf16[14,14,4,512]{3,2,1,0:T(4,128)(2,1)S(1)}, bf16[14,14,4,512]{3,2,1,0:T(4,128)(2,1)}, u32[]{:S(2)}) copy-start(bf16[14,14,4,512]{3,2,1,0:T(4,128)(2,1)} %get-tuple-element.47) | copy-start | bytes 2408452
  175.7 1.7 copy-start.1

commit v5 on v4

--- a/solution.py
+++ b/solution.py
@@ -981,7 +981,7 @@
             whole((1, C)),
             whole((1, 4 * C)),
         ],
-        compiler_params=pltpu.CompilerParams(vmem_limit_bytes=32 * MIB),
+        compiler_params=pltpu.CompilerParams(vmem_limit_bytes=60 * MIB),
         name="spread",
     )(*[totals] * 7)
 

time: 179 us -> 179 us (level)
  Pallas kernels: 172 us -> 175 us
  local copies, waits for them, and re-layouts: 4.82 us -> 2.93 us
    pallas_call x1, Pallas kernels: 2.86 us -> 4.93 us  [run_spread(): pl.pallas_call(spread_kernel, grid=(4,), out_shape=[jax.ShapeDtypeStruct(...]
    unnamed x8 -> x6, local copies, waits for them, and re-layouts: 4.74 us -> 2.85 us
where the time goes in v5:
time: 179 us
  Pallas kernels  175 us (98%)
  local copies, waits for them, and re-layouts  2.93 us (2%)
    pallas_call x1, Pallas kernels, run_backward(): pl.pallas_call(lambda *refs: backward_kernel(dims, *refs), grid=(16,), ou...  95.4 us
    pallas_call x1, Pallas kernels, run_forward(): pl.pallas_call(forward_kernel, grid=(10,), out_shape=[jax.ShapeDtypeStruc...  74.2 us
    pallas_call x1, Pallas kernels, run_spread(): pl.pallas_call(spread_kernel, grid=(4,), out_shape=[jax.ShapeDtypeStruct(...  4.93 us

profile of v5, /device:TPU:1, one launch (start us, length us, event | category | flops | bytes accessed | tf_op | source)
XLA Modules:
  0.0 178.8 jit_solution(7016228829334275733)
XLA Ops:
  0.7 0.1 pad.3.clone
  0.8 0.7 add_convert_fusion.pos
  1.4 74.2 %forward.1 = (bf16[8,392,256]{2,1,0:T(8,128)(2,1)}, bf16[8,768,392]{2,1,0:T(8,128)(2,1)}, bf16[8,8,392,392]{3,2,1,0:T(8,128)(2,1)}, f32[8,8,392]{2,1,0:T(8,128)}...) custom-call(bf16[7,28,16,256]{3,2,1,0:T(8,128)(2,1)} %bitcast.19, ...), custom_call_target="tpu_custom_call" | custom-call | tf_op jit(solution)/shard_map/forward/pallas_call | solution.py:448
  75.6 95.4 %backward.1 = (bf16[12288,128]{1,0:T(8,128)(2,1)}, bf16[14,14,4,512]{3,2,1,0:T(4,128)(2,1)}, bf16[7,28,16,256]{3,2,1,0:T(8,128)(2,1)}) custom-call(bf16[8,392,256]{2,1,0:T(8,128)(2,1)} %get-tuple-element.34.refs_0_, bf16[8,256,392]{2,1,0:T(8,128)(2,1)} %get-tuple-element.35.refs_1_.refs_8_, bf16[8,392,256]{2,1,0:T(8,128)(2,1)} %get-tuple-element.36.refs_2_, ...), custom_call_target="tpu_custom_call" | custom-call | tf_op jit(solution)/shard_map/backward/pallas_call | solution.py:899
  171.0 0.0 copy-start.1
  171.0 4.9 %spread.1 = (f32[256,768]{1,0:T(8,128)}, f32[256,256]{1,0:T(8,128)}, f32[256,1024]{1,0:T(8,128)}, f32[1024,256]{1,0:T(8,128)}, f32[1024,512]{1,0:T(8,128)}, /*in...) custom-call(bf16[48,256,128]{2,1,0:T(8,128)(2,1)} %bitcast.12, bf16[48,256,128]{2,1,0:T(8,128)(2,1)} %bitcast.13, ...), custom_call_target="tpu_custom_call" | custom-call | tf_op jit(solution)/shard_map/spread/pallas_call | solution.py:966
  176.0 0.0 copy-start
  176.0 0.0 copy-done.1
  176.0 0.9 copy.23
  176.9 0.8 copy-done
  177.7 1.2 copy.24
  (3 shorter events, 0.0 us)
Async XLA Ops:
  171.0 5.0 %copy-start.1 = (bf16[14,14,4,512]{3,2,1,0:T(4,128)(2,1)S(1)}, bf16[14,14,4,512]{3,2,1,0:T(4,128)(2,1)}, u32[]{:S(2)}) copy-start(bf16[14,14,4,512]{3,2,1,0:T(4,128)(2,1)} %get-tuple-element.47) | copy-start | bytes 2408452
  176.0 1.7 copy-start
